TPU v7x, 256 devices: a whole 4x4x8 slice. The times are simulated.
256 devices in a mesh: expert: 32 (over x, z), replica: 4 (over y), tensor: 2 (over core).
Axes of the slice: x: 4, y: 4, z: 8, core: 2. Of those that a mesh axis runs over, the one named last changes fastest.
Arguments:
- grad_out: bfloat16 [16384, 3584], P(('expert', 'replica')), may hold values from -6 to 6
- gates: float32 [16384, 4], P(('expert', 'replica')), may hold values from 0.1 to 1
- expert_ids: int32 [16384, 4], P(('expert', 'replica')), may hold values from 0 to 31, all different within a row; in each aligned block of 128 rows (0 to 127, 128 to 255, ...) at most 24 rows name the same one
- gate_pre: bfloat16 [32, 3072, 1024], P('expert', 'replica', 'tensor'), may hold values from -6 to 6
- up_pre: bfloat16 [32, 3072, 1024], P('expert', 'replica', 'tensor'), may hold values from -6 to 6
- w_gate: bfloat16 [32, 3584, 1024], P('expert', 'replica', 'tensor'), may hold values from -0.09375 to 0.09375
- w_up: bfloat16 [32, 3584, 1024], P('expert', 'replica', 'tensor'), may hold values from -0.09375 to 0.09375
- w_down: bfloat16 [32, 3584, 1024], P('expert', 'replica', 'tensor'), may hold values from -0.09375 to 0.09375
- residual: bfloat16 [32, 14336, 1024], P('expert', 'replica', 'tensor'), may hold values from -6 to 6
Outputs:
- grad_in: bfloat16 [16384, 3584], P(('expert', 'replica'), 'tensor')
- code_sums: float32 [32, 3584, 1024], P('expert', 'replica', 'tensor')
- block_scales: float32 [32, 28, 1024], P('expert', None, 'tensor')
Inputs may be any that keep to these rules, and one draw needn't show every extreme that they name: `expert_ids`: among the 128 tokens of one device no expert is named more than 24 times, and in every draw some device names some expert exactly 24 times; a token names 4 different experts.
All inputs are finite; a program needn't handle non-finite values.
Results may differ from a plain program's by a relative error of at most 0.017.
Values may be sent and summed in bfloat16 or wider, within the bound.
A program may use at most 128 MiB of HBM per device.

v0:
```python
import jax
import jax.numpy as jnp
from jax import lax
from jax.sharding import PartitionSpec as P

BLOCK = 128


def contract_rows(left, right):
    return lax.dot_general(
        left, right, (((1,), (1,)), ((), ())), preferred_element_type=jnp.float32
    )


def local(grad_out, gates, expert_ids, gate_pre, up_pre, w_gate, w_up, w_down, residual):
    expert_count = lax.axis_size("expert")
    slot_count = gate_pre.shape[1]
    capacity = slot_count // expert_count
    model_width = grad_out.shape[1]
    top_count = expert_ids.shape[1]
    pick_count = expert_ids.shape[0] * top_count
    group_width = gate_pre.shape[2]
    flat_ids = expert_ids.reshape(pick_count)
    onehot = (flat_ids[:, None] == jnp.arange(expert_count, dtype=jnp.int32)[None, :]).astype(
        jnp.int32
    )
    earlier = jnp.cumsum(onehot, axis=0) - onehot
    slot_index = jnp.sum(earlier * onehot, axis=1)
    target = flat_ids * capacity + slot_index
    slot_owner = (
        jnp.full((slot_count,), -1, jnp.int32)
        .at[target]
        .set(jnp.arange(pick_count, dtype=jnp.int32))
    )
    filled = (slot_owner >= 0).astype(jnp.float32)
    chosen = jnp.maximum(slot_owner, 0)
    weight = gates.reshape(pick_count)[chosen] * filled
    outgoing = (grad_out[chosen // top_count].astype(jnp.float32) * weight[:, None]).astype(
        jnp.bfloat16
    )
    received = lax.all_to_all(
        outgoing.reshape(expert_count, capacity, model_width),
        "expert",
        split_axis=0,
        concat_axis=0,
        tiled=True,
    )
    received = received.reshape(slot_count, model_width)
    act_gate = gate_pre[0].astype(jnp.float32)
    act_up = up_pre[0].astype(jnp.float32)
    sigmoid_gate = jax.nn.sigmoid(act_gate)
    silu_gate = act_gate * sigmoid_gate
    hidden = (silu_gate * act_up).astype(jnp.bfloat16)
    full_gate, full_up, full_down = (
        lax.all_gather(w_gate, "replica", axis=1, tiled=True),
        lax.all_gather(w_up, "replica", axis=1, tiled=True),
        lax.all_gather(w_down, "replica", axis=1, tiled=True),
    )
    hidden_grad = jnp.dot(received, full_down[0], preferred_element_type=jnp.float32)
    gate_grad = (
        hidden_grad * act_up * sigmoid_gate * (1.0 + act_gate * (1.0 - sigmoid_gate))
    ).astype(jnp.bfloat16)
    up_grad = (hidden_grad * silu_gate).astype(jnp.bfloat16)
    partial_value = contract_rows(gate_grad, full_gate[0]) + contract_rows(up_grad, full_up[0])
    stacked = partial_value.astype(jnp.bfloat16).reshape(expert_count, capacity, 1, model_width)
    arrived = lax.all_to_all(
        lax.all_to_all(stacked, "expert", split_axis=0, concat_axis=0, tiled=True),
        "tensor",
        split_axis=3,
        concat_axis=2,
        tiled=True,
    )
    returned = jnp.sum(arrived.astype(jnp.float32), axis=2).astype(jnp.bfloat16)
    returned_rows = returned.reshape(slot_count, returned.shape[2])
    picked_rows = (
        returned_rows[target]
        .astype(jnp.float32)
        .reshape(pick_count // top_count, top_count, returned_rows.shape[1])
    )
    grad_in = jnp.sum(picked_rows, axis=1).astype(jnp.bfloat16)
    weight_grad = lax.dot_general(
        received, hidden, (((0,), (0,)), ((), ())), preferred_element_type=jnp.float32
    )
    corrected = weight_grad + residual[0].astype(jnp.float32)
    block_count = model_width // BLOCK
    local_max = jnp.max(jnp.abs(corrected).reshape(block_count, BLOCK, group_width), axis=1)
    block_scales = (
        lax.pmax(local_max.astype(jnp.bfloat16), "replica").astype(local_max.dtype) + 1e-06
    )
    codes = (corrected.reshape(block_count, BLOCK, group_width) / block_scales[:, None, :]).reshape(
        model_width, group_width
    )
    code_sums = lax.psum_scatter(
        codes.astype(jnp.bfloat16), "replica", scatter_dimension=0, tiled=True
    ).astype(jnp.float32)
    return (grad_in, code_sums[None], block_scales[None])


def solution(mesh):
    in_specs = (
        P(("expert", "replica"), None),
        P(("expert", "replica"), None),
        P(("expert", "replica"), None),
        P("expert", "replica", "tensor"),
        P("expert", "replica", "tensor"),
        P("expert", "replica", "tensor"),
        P("expert", "replica", "tensor"),
        P("expert", "replica", "tensor"),
        P("expert", "replica", "tensor"),
    )
    out_specs = (
        P(("expert", "replica"), "tensor"),
        P("expert", "replica", "tensor"),
        P("expert", None, "tensor"),
    )
    return jax.shard_map(local, mesh=mesh, in_specs=in_specs, out_specs=out_specs, check_vma=False)
```

profile of v0, /device:TPU:1, one launch (start us, length us, event | category | flops | bytes accessed | tf_op | source)
XLA Modules:
  0.0 477.0 jit_solution(862607357198689776)
XLA Ops:
  14.8 5.0 %gather_fusion.1 = f32[768]{0:T(1024)S(1)} fusion(f32[512]{0:T(512)S(1)} %reshape.94, s32[1024]{0:T(1024)S(1)} %get-tuple-element.7), kind=kCustom, calls=%fused_computation.1 | custom fusion | bytes 9216 | tf_op jit(solution)/shard_map/gather | solution.py:37
  19.9 5.5 %gather_fusion = bf16[768,3584]{1,0:T(8,128)(2,1)} fusion(bf16[128,3584]{1,0:T(8,128)(2,1)S(1)} %copy-done, s32[1024]{0:T(1024)S(1)} %get-tuple-element.8), kind=kCustom, calls=%fused_computation | custom fusion | bytes 11013120 | tf_op jit(solution)/shard_map/gather | solution.py:38
  25.4 7.1 %fusion = bf16[32,24,3584]{2,1,0:T(8,128)(2,1)} fusion(bf16[32,24,3584]{2,1,0:T(8,128)(2,1)} %bitcast.101, f32[32,24]{1,0:T(8,128)S(1)} %mul.63), kind=kLoop, calls=%fused_computation.5 | loop fusion | flops 8257536 | bytes 11013120 | tf_op jit(solution)/shard_map/convert_element_type | solution.py:38
  32.5 11.8 %all-to-all-start = ((bf16[32,24,3584]{2,1,0:T(8,128)(2,1)}), bf16[32,24,3584]{2,1,0:T(8,128)(2,1)}, u32[]{:S(2)}, u32[]{:S(2)}) async-start(bf16[32,24,3584]{2,1,0:T(8,128)(2,1)} %fusion), calls=%async_computation | async-start | bytes 11010048 | tf_op jit(solution)/shard_map/all_to_all | solution.py:41
  45.8 14.4 %all-gather.4.cloned.1.call-done = bf16[1,3584,512]{2,1,0:T(8,128)(2,1)} async-done(((bf16[1,896,512]{2,1,0:T(8,128)(2,1)}), bf16[1,3584,512]{2,1,0:T(8,128)(2,1)}) %all-gather.4.cloned.1.call-update) | async-done | bytes 3670032 | tf_op jit(solution)/shard_map/all_gather | solution.py:57
  60.1 107.0 %all-to-all-done = bf16[32,24,3584]{2,1,0:T(8,128)(2,1)} async-done(((bf16[32,24,3584]{2,1,0:T(8,128)(2,1)}), bf16[32,24,3584]{2,1,0:T(8,128)(2,1)}, u32[]{:S(2)}, u32[]{:S(2)}) %all-to-all-start) | async-done | bytes 5505056 | tf_op jit(solution)/shard_map/all_to_all | solution.py:41
  167.1 6.2 %fusion.5 = f32[768,512]{1,0:T(8,128)S(1)} fusion(bf16[768,3584]{1,0:T(8,128)(2,1)} %bitcast.4, bf16[1,3584,512]{2,1,0:T(8,128)(2,1)} %all-gather.4.cloned.1.call-done), kind=kOutput, calls=%fused_computation.13 | convolution fusion | flops 2818572288 | bytes 10747904 | tf_op jit(solution)/shard_map/dot_general | solution.py:59
  173.4 8.1 %fusion.3 = f32[768,3584]{1,0:T(8,128)} fusion(bf16[1,3584,512]{2,1,0:T(8,128)(2,1)} %all-gather.6.cloned.1.call-done, f32[768,512]{1,0:T(8,128)S(1)} %fusion.5, bf16[1,768,512]{2,1,0:T(8,128)(2,1)S(1)} %copy-done.2, bf16[1,768,512]{2,1,0:T(8,128)(2,1)S(1)} %copy-done.3), kind=kOutput, calls=%fused_computation.11 | convolution fusion | flops 2823290880 | bytes 17825792 | tf_op jit(solution)/shard_map/dot_general | solution.py:10
  181.4 8.6 %add_convert_fusion = bf16[768,3584]{1,0:T(8,128)(2,1)} fusion(f32[768,3584]{1,0:T(8,128)} %fusion.3, bf16[1,3584,512]{2,1,0:T(8,128)(2,1)} %all-gather.8.cloned.1.call-done, f32[768,512]{1,0:T(8,128)S(1)} %fusion.5, bf16[1,768,512]{2,1,0:T(8,128)(2,1)S(1)} %copy-done.3), kind=kOutput, calls=%fused_computation.6 | convolution fusion | flops 2826829824 | bytes 22544384 | tf_op jit(solution)/shard_map/dot_general | solution.py:10
  190.0 8.2 %all-to-all-start.1 = ((bf16[32,24,1,3584]{3,1,2,0:T(8,128)(2,1)}), bf16[32,24,1,3584]{3,1,2,0:T(8,128)(2,1)}, u32[]{:S(2)}, u32[]{:S(2)}) async-start(bf16[32,24,1,3584]{3,1,2,0:T(8,128)(2,1)} %bitcast.102), calls=%async_computation.1 | async-start | bytes 11010048 | tf_op jit(solution)/shard_map/all_to_all | solution.py:67
  198.5 9.2 %fusion.40 = (bf16[3584,512]{1,0:T(8,128)(2,1)}, f32[3584,512]{1,0:T(8,128)}) fusion(bf16[1,3584,512]{2,1,0:T(8,128)(2,1)} %param.17, bf16[768,3584]{1,0:T(8,128)(2,1)} %bitcast.4, bf16[1,768,512]{2,1,0:T(8,128)(2,1)S(1)} %copy-done.2, bf16[1,768,512]{2,1,0:T(8,128)(2,1)S(1)} %copy-done.3), kind=kOutput, calls=%fused_computation.68 | convolution fusion | flops 2829058048 | bytes 21757952 | tf_op jit(solution)/shard_map/dot_general | solution.py:81
  210.4 15.1 %pmax.7 = bf16[28,512]{1,0:T(8,128)(2,1)S(1)} all-reduce(bf16[28,512]{1,0:T(8,128)(2,1)S(1)} %reduce_max.9), channel_id=1, replica_groups=mesh['expert'=32,'replica'=4,'tensor'=2] {'replica'}, use_global_device_ids=true, to_apply=%region_7.8 | all-reduce | flops 14336 | bytes 57344 | tf_op jit(solution)/shard_map/pmax | solution.py:88
  225.5 6.0 %fusion.1 = bf16[3584,512]{1,0:T(8,128)(2,1)} fusion(f32[3584,512]{1,0:T(8,128)} %get-tuple-element.6, f32[28,512]{1,0:T(8,128)S(1)} %convert_add_fusion.1), kind=kLoop, calls=%fused_computation.9 | loop fusion | flops 3670016 | bytes 11067392 | tf_op jit(solution)/shard_map/convert_element_type | solution.py:94
  232.2 46.6 %reduce-scatter.2.cloned.1.call-done = bf16[896,512]{1,0:T(8,128)(2,1)} async-done(((bf16[3584,512]{1,0:T(8,128)(2,1)}), bf16[896,512]{1,0:T(8,128)(2,1)}) %reduce-scatter.2.cloned.1.call-update) | async-done | bytes 917520 | tf_op jit(solution)/shard_map/reduce_scatter | solution.py:93
  278.7 2.7 bitcast_convert_fusion
  281.4 39.6 %all-to-all-done.1 = bf16[32,24,1,3584]{3,1,2,0:T(8,128)(2,1)} async-done(((bf16[32,24,1,3584]{3,1,2,0:T(8,128)(2,1)}), bf16[32,24,1,3584]{3,1,2,0:T(8,128)(2,1)}, u32[]{:S(2)}, u32[]{:S(2)}) %all-to-all-start.1) | async-done | bytes 5505056 | tf_op jit(solution)/shard_map/all_to_all | solution.py:67
  321.0 22.9 %copy.30 = bf16[32,24,1,3584]{0,1,2,3:T(8,128)(2,1)} copy(bf16[32,24,1,3584]{3,1,2,0:T(8,128)(2,1)} %all-to-all-done.1) | data formatting | bytes 11010048 | tf_op jit(solution)/shard_map/all_to_all | solution.py:67
  343.9 31.8 %reshape.141 = bf16[2,2,688128]{2,1,0:T(2,128)(2,1)} reshape(bf16[3584,1,24,32]{3,2,1,0:T(8,128)(2,1)} %bitcast.100) | data formatting | bytes 11010048
  375.7 23.5 %all_to_all.22 = bf16[2,2,688128]{2,1,0:T(2,128)(2,1)} all-to-all(bf16[2,2,688128]{2,1,0:T(2,128)(2,1)} %reshape.141), channel_id=1, replica_groups=mesh['expert'=32,'replica'=4,'tensor'=2] {'tensor'}, dimensions={0} | all-to-all | bytes 11010048 | tf_op jit(solution)/shard_map/all_to_all | solution.py:66
  399.2 23.1 %reshape.142 = bf16[3584,1,24,32]{3,2,1,0:T(8,128)(2,1)} reshape(bf16[2,2,688128]{2,1,0:T(2,128)(2,1)} %all_to_all.22) | data formatting | bytes 11010048
  422.3 20.8 %reduce_sum.37 = bf16[32,24,1792]{0,1,2:T(8,128)(2,1)} reduce(bf16[32,24,2,1792]{0,1,3,2:T(8,128)(2,1)} %bitcast.99, bf16[]{:T(256)} %constant.43.clone.1), dimensions={2}, to_apply=%region_4.5 | reduce | flops 1376256 | bytes 8257538 | tf_op jit(solution)/shard_map/reduce_sum | solution.py:73
  443.0 14.8 %copy.32 = bf16[32,24,1792]{2,1,0:T(8,128)(2,1)} copy(bf16[32,24,1792]{0,1,2:T(8,128)(2,1)} %reduce_sum.37) | data formatting | bytes 5505024 | tf_op jit(solution)/shard_map/reduce_sum | solution.py:73
  457.9 6.2 %gather_fusion.2 = bf16[512,1792]{1,0:T(8,128)(2,1)S(1)} fusion(bf16[768,1792]{1,0:T(8,128)(2,1)} %bitcast.98, s32[1024]{0:T(1024)S(1)} %pad_clamp_fusion), kind=kCustom, calls=%fused_computation.2 | custom fusion | bytes 3672064 | tf_op jit(solution)/shard_map/gather | solution.py:76
  465.7 4.5 reduce_sum.38
  (44 shorter events, 14.4 us)
Async XLA Ops:
  7.2 12.7 %copy-start = (bf16[128,3584]{1,0:T(8,128)(2,1)S(1)}, bf16[128,3584]{1,0:T(8,128)(2,1)}, u32[]{:S(2)}) copy-start(bf16[128,3584]{1,0:T(8,128)(2,1)} %param.9) | copy-start | bytes 2752516
  7.2 53.0 %all-gather.4.cloned.1.call-start = ((), (), s32[]{:S(2)}) async-start(), calls=%async_computation.4 | async-start | bytes 4587520 | tf_op jit(solution)/shard_map/all_gather | solution.py:57
  32.5 134.7 %all-to-all-start = ((bf16[32,24,3584]{2,1,0:T(8,128)(2,1)}), bf16[32,24,3584]{2,1,0:T(8,128)(2,1)}, u32[]{:S(2)}, u32[]{:S(2)}) async-start(bf16[32,24,3584]{2,1,0:T(8,128)(2,1)} %fusion), calls=%async_computation | async-start | bytes 11010048 | tf_op jit(solution)/shard_map/all_to_all | solution.py:41
  44.3 129.0 %all-gather.6.cloned.1.call-start = ((), (), s32[]{:S(2)}) async-start(), calls=%async_computation.5 | async-start | bytes 4587520 | tf_op jit(solution)/shard_map/all_gather | solution.py:55
  45.0 136.4 %all-gather.8.cloned.1.call-start = ((), (), s32[]{:S(2)}) async-start(), calls=%async_computation.6 | async-start | bytes 4587520 | tf_op jit(solution)/shard_map/all_gather | solution.py:56
  167.1 6.2 %copy-start.2 = (bf16[1,768,512]{2,1,0:T(8,128)(2,1)S(1)}, bf16[1,768,512]{2,1,0:T(8,128)(2,1)}, u32[]{:S(2)}) copy-start(bf16[1,768,512]{2,1,0:T(8,128)(2,1)} %param.13) | copy-start | bytes 2359300
  167.1 6.2 %copy-start.3 = (bf16[1,768,512]{2,1,0:T(8,128)(2,1)S(1)}, bf16[1,768,512]{2,1,0:T(8,128)(2,1)}, u32[]{:S(2)}) copy-start(bf16[1,768,512]{2,1,0:T(8,128)(2,1)} %param.12) | copy-start | bytes 2359300
  190.0 131.0 %all-to-all-start.1 = ((bf16[32,24,1,3584]{3,1,2,0:T(8,128)(2,1)}), bf16[32,24,1,3584]{3,1,2,0:T(8,128)(2,1)}, u32[]{:S(2)}, u32[]{:S(2)}) async-start(bf16[32,24,1,3584]{3,1,2,0:T(8,128)(2,1)} %bitcast.102), calls=%async_computation.1 | async-start | bytes 11010048 | tf_op jit(solution)/shard_map/all_to_all | solution.py:67
  198.2 80.5 %reduce-scatter.2.cloned.1.call-start = ((), (), s32[]{:S(2)}) async-start(), calls=%async_computation.7 | async-start | bytes 4587520 | tf_op jit(solution)/shard_map/reduce_scatter | solution.py:93
  457.8 12.3 %copy-start.1 = (bf16[128,3584]{1,0:T(8,128)(2,1)S(1)}, bf16[128,3584]{1,0:T(8,128)(2,1)}, u32[]{:S(2)}) copy-start(bf16[128,3584]{1,0:T(8,128)(2,1)} %param.9) | copy-start | bytes 2752516
Sparse Core Ops, SparseCore 0:
  9.8 50.2 all-gather.3
  62.0 46.7 all-gather.5
  110.6 46.7 all-gather.7
  231.6 47.0 reduce-scatter.1
where the time goes:
time: 482 us; the launch traced here: 477 us
  waiting for transfers between devices  210 us (44%)
  local copies, waits for them, and re-layouts  117 us (24%)
  other arithmetic  45.6 us (9%)
  blocking collectives  38.6 us (8%)
  matrix products  32 us (7%)
  starting transfers between devices  20.4 us (4%)
  between operations  14.2 us (3%)
    all_to_all x1, waiting for transfers between devices, local(): lax.all_to_all(outgoing.reshape(expert_count, capacity, model_width), 'ex...  107 us
    unnamed x12, local copies, waits for them, and re-layouts  56.5 us
    reduce_scatter x1, waiting for transfers between devices, local(): lax.psum_scatter(codes.astype(jnp.bfloat16), 'replica', scatter_dimension...  46.6 us
    all_to_all x1, waiting for transfers between devices, local(): lax.all_to_all(stacked, 'expert', split_axis=0, concat_axis=0, tiled=True)  39.6 us
    all_to_all x1, blocking collectives, local(): lax.all_to_all(lax.all_to_all(stacked, 'expert', split_axis=0, concat_axi...  23.5 us
    all_to_all x1, local copies, waits for them, and re-layouts, local(): lax.all_to_all(stacked, 'expert', split_axis=0, concat_axis=0, tiled=True)  22.9 us
    reduce_sum x1, other arithmetic, local(): returned = jnp.sum(arrived.astype(jnp.float32), axis=2).astype(jnp.bfloat16)  20.8 us
    dot_general x2, matrix products, contract_rows(): lax.dot_general(left, right, (((1,), (1,)), ((), ())), preferred_element_...  16.6 us
  transfers between devices with their start and end apart: 6, of which 4 were waited for; matrix products, arithmetic and copies ran while one was open for 13% of the time, Pallas kernels for 0%

commit v1 on v0

v1 whole, which is shorter than its diff:
```python
import jax
import jax.numpy as jnp
from jax import lax
from jax.experimental import pallas as pl
from jax.experimental.pallas import tpu as pltpu
from jax.sharding import PartitionSpec as P

MESH = pl.DeviceIdType.MESH
BF16, F32 = jnp.bfloat16, jnp.float32

EXPERTS, REPLICAS = 32, 4
TOKENS, TOP, CAP = 128, 4, 24
D, GROUP, SHARD, BLOCK = 3584, 512, 896, 128
HALF_D = D // 2
ROWS_A, ROWS_B = EXPERTS * 16, EXPERTS * 8
SLOTS = ROWS_A + ROWS_B
WIDE = 3 * SHARD
CUT = SHARD // 2


def dot(a, b, dims=((1,), (0,))):
    return lax.dot_general(a, b, (dims, ((), ())), preferred_element_type=F32)


def kernel(
    ids_ref, gates_ref, grad_hbm, gate_hbm, up_hbm, wg_hbm, wu_hbm, wd_hbm, res_hbm,
    grad_in_ref, sums_ref, scales_ref,
    out, rcv, ret, part_send, part_got, part_own, wf, routed_b, pick, pick_t, grad, gate_pre, up_pre,
    hid, fac_gate, fac_up, gate_grad, up_grad, res, corr, code_got, maxima,
    a_send, a_recv, f_send, f_recv, r_send, r_recv, w_send, w_recv, p_send, p_recv,
    m_send, m_recv, c_send, c_recv, l_sem,
):
    me = lax.axis_index("expert")
    y = lax.axis_index("replica")
    core = lax.axis_index("tensor")
    other = 1 - core
    right, left, opposite = lax.rem(y + 1, 4), lax.rem(y + 3, 4), lax.rem(y + 2, 4)
    weights = (wd_hbm, wg_hbm, wu_hbm)

    def local_copies():
        copies = [
            pltpu.make_async_copy(
                grad_hbm.at[:, pl.ds(pl.multiple_of(core * HALF_D, HALF_D), HALF_D)], grad, l_sem.at[0]
            ),
            pltpu.make_async_copy(gate_hbm, gate_pre, l_sem.at[1]),
            pltpu.make_async_copy(up_hbm, up_pre, l_sem.at[2]),
            pltpu.make_async_copy(res_hbm, res, l_sem.at[3]),
        ]
        for w in range(3):
            copies.append(pltpu.make_async_copy(weights[w], wf.at[w, y], l_sem.at[4 + w]))
        return copies

    locals_ = local_copies()
    for copy in locals_:
        copy.start()

    barrier = pltpu.get_barrier_semaphore()

    def greet(i, _):
        pl.semaphore_signal(
            barrier, inc=1, device_id={"expert": lax.rem(me + i, EXPERTS)}, device_id_type=MESH
        )
        return 0

    lax.fori_loop(1, EXPERTS, greet, 0)
    for peer in (right, left, opposite):
        pl.semaphore_signal(barrier, inc=1, device_id={"replica": peer}, device_id_type=MESH)
    pl.semaphore_signal(barrier, inc=1, device_id={"tensor": other}, device_id_type=MESH)

    ids = ids_ref[...].astype(F32)
    expert_row = lax.broadcasted_iota(jnp.int32, (EXPERTS, TOKENS), 0).astype(F32)
    named = jnp.zeros((EXPERTS, TOKENS), F32)
    for k in range(TOP):
        named = named + jnp.where(ids[k : k + 1, :] == expert_row, 1.0, 0.0)
    before = jnp.where(
        lax.broadcasted_iota(jnp.int32, (TOKENS, TOKENS), 0)
        < lax.broadcasted_iota(jnp.int32, (TOKENS, TOKENS), 1),
        1.0,
        0.0,
    ).astype(BF16)
    earlier = dot(named.astype(BF16), before)
    keys = []
    for k in range(TOP):
        id_k = ids[k : k + 1, :]
        slot_k = jnp.sum(jnp.where(id_k == expert_row, earlier, 0.0), axis=0, keepdims=True)
        keys.append(id_k * 32.0 + slot_k)
    row = lax.broadcasted_iota(jnp.int32, (ROWS_A, 1), 0)
    in_row = lax.rem(row, 16)
    base = (row - in_row) * 2
    key_a = (base + in_row).astype(F32)
    key_b = (base + 16 + lax.rem(row, 8)).astype(F32)
    lower = in_row < 8
    hot = jnp.zeros((ROWS_A, TOKENS), F32)
    weigh = jnp.zeros((ROWS_A, TOKENS), F32)
    hot_b = jnp.zeros((ROWS_A, TOKENS), F32)
    weigh_b = jnp.zeros((ROWS_A, TOKENS), F32)
    for k in range(TOP):
        same = key_a == keys[k]
        same_b = key_b == keys[k]
        gate_k = gates_ref[k : k + 1, :]
        hot = hot + jnp.where(same, 1.0, 0.0)
        weigh = weigh + jnp.where(same, gate_k, 0.0)
        hot_b = hot_b + jnp.where(same_b, 1.0, 0.0)
        weigh_b = weigh_b + jnp.where(same_b, gate_k, 0.0)
    gate_a = jnp.sum(weigh, axis=1, keepdims=True)
    gate_b = jnp.sum(weigh_b, axis=1, keepdims=True)
    hot_b0 = jnp.where(lower, hot_b, 0.0)
    hot_b1 = jnp.where(lower, 0.0, hot_b)
    pick[0] = hot.astype(BF16)
    pick[1] = hot_b0.astype(BF16)
    pick[2] = hot_b1.astype(BF16)

    def weight_copy(w, i):
        peer, lo = ((right, 0), (left, CUT), (right, CUT), (left, 0))[i]
        return pltpu.make_async_remote_copy(
            src_ref=weights[w].at[pl.ds(lo, CUT)],
            dst_ref=wf.at[w, y, pl.ds(lo, CUT)],
            send_sem=w_send.at[w * 6 + i],
            recv_sem=w_recv.at[w * 6 + i],
            device_id={"replica": peer},
            device_id_type=MESH,
        )

    def weight_relay(w, i):
        peer, owner, lo = ((right, left, 0), (left, right, CUT))[i]
        block = wf.at[w, owner, pl.ds(lo, CUT)]
        return pltpu.make_async_remote_copy(
            src_ref=block,
            dst_ref=block,
            send_sem=w_send.at[w * 6 + 4 + i],
            recv_sem=w_recv.at[w * 6 + 4 + i],
            device_id={"replica": peer},
            device_id_type=MESH,
        )

    def relay(w):
        for i in range(2):
            weight_copy(w, i).wait_recv()
            weight_relay(w, i).start()

    def weight_ready(w):
        locals_[4 + w].wait()
        for i in (2, 3):
            weight_copy(w, i).wait_recv()
        for i in range(2):
            weight_relay(w, i).wait_recv()

    pl.semaphore_wait(barrier, EXPERTS + 3)
    for w in range(3):
        for i in range(4):
            weight_copy(w, i).start()

    locals_[0].wait()
    for q in range(4):
        rows = pl.ds(q * 128, 128)
        block = dot(pick[0, rows, :], grad[...]) * gate_a[q * 128 : (q + 1) * 128]
        out[pl.ds(q * 8, 8), :, 0:HALF_D] = block.astype(BF16).reshape(8, 16, HALF_D)
        block = dot(pick[1, rows, :], grad[:, 0:SHARD]) + dot(pick[2, rows, :], grad[:, SHARD:HALF_D])
        block = block * gate_b[q * 128 : (q + 1) * 128]
        out[pl.ds(q * 8, 8), :, HALF_D:WIDE] = block.astype(BF16).reshape(8, 16, SHARD)

    def dispatch(i):
        peer = lax.rem(me + i, EXPERTS)
        return pltpu.make_async_remote_copy(
            src_ref=out.at[peer],
            dst_ref=rcv.at[core, me],
            send_sem=a_send.at[i],
            recv_sem=a_recv.at[i],
            device_id={"expert": peer},
            device_id_type=MESH,
        )

    def share(i):
        source = lax.rem(me + EXPERTS - i, EXPERTS)
        return pltpu.make_async_remote_copy(
            src_ref=rcv.at[core, source],
            dst_ref=rcv.at[core, source],
            send_sem=f_send.at[i],
            recv_sem=f_recv.at[i],
            device_id={"tensor": other},
            device_id_type=MESH,
        )

    def start_dispatch(i, _):
        dispatch(i).start()
        return 0

    lax.fori_loop(1, EXPERTS, start_dispatch, 0)
    own = pltpu.make_async_copy(out.at[me], rcv.at[core, me], l_sem.at[7])
    own.start()

    locals_[1].wait()
    locals_[2].wait()

    def activate(g, _):
        rows = pl.ds(pl.multiple_of(g * 192, 192), 192)
        a = gate_pre[rows, :].astype(F32).reshape(8, CAP, GROUP)
        u = up_pre[rows, :].astype(F32).reshape(8, CAP, GROUP)
        for lo, hi, at in ((0, 16, g * 128), (16, 24, ROWS_A + g * 64)):
            n = 8 * (hi - lo)
            a_part = a[:, lo:hi].reshape(n, GROUP)
            u_part = u[:, lo:hi].reshape(n, GROUP)
            sigma = 1.0 / (1.0 + jnp.exp(-a_part))
            silu = a_part * sigma
            to = pl.ds(pl.multiple_of(at, 64), n)
            hid[to, :] = (silu * u_part).astype(BF16)
            fac_up[to, :] = silu
            fac_gate[to, :] = u_part * sigma * (1.0 + a_part * (1.0 - sigma))
        return 0

    lax.fori_loop(0, 4, activate, 0)
    for j in range(3):
        pick_t[j] = jnp.transpose(pick[j].astype(F32)).astype(BF16)

    own.wait()
    share(0).start()

    def pass_on(i, _):
        dispatch(i).wait_recv()
        share(i).start()
        return 0

    relay(0)
    lax.fori_loop(1, 12, pass_on, 0)
    relay(1)
    lax.fori_loop(12, 24, pass_on, 0)
    relay(2)
    lax.fori_loop(24, EXPERTS, pass_on, 0)

    def share_got(i, _):
        share(i).wait()
        return 0

    lax.fori_loop(0, EXPERTS, share_got, 0)

    for h in range(2):
        for q in range(2):
            def unfold(g, _, h=h, q=q):
                raw = rcv[h, pl.ds(g * 8, 8), :, HALF_D:WIDE].astype(F32)
                rows = raw.reshape(8, 2, 8, SHARD)[:, q].reshape(64, SHARD)
                routed_b[h, pl.ds(pl.multiple_of(g * 64, 64), 64), q * SHARD : (q + 1) * SHARD] = rows.astype(BF16)
                return 0

            lax.fori_loop(0, 4, unfold, 0)

    def w_half(w, h):
        return wf[w, pl.ds(2 * h, 2)].reshape(HALF_D, GROUP)

    weight_ready(0)

    def grads(at, total):
        rows = pl.ds(pl.multiple_of(at, 256), 256)
        gate_grad[rows, :] = (total * fac_gate[rows, :]).astype(BF16)
        up_grad[rows, :] = (total * fac_up[rows, :]).astype(BF16)

    def rows_a(t, _):
        total = jnp.zeros((256, GROUP), F32)
        for h in range(2):
            x = rcv[h, pl.ds(t * 16, 16), :, 0:HALF_D].reshape(256, HALF_D)
            total = total + dot(x, w_half(0, h))
        grads(t * 256, total)
        return 0

    lax.fori_loop(0, 2, rows_a, 0)
    grads(ROWS_A, dot(routed_b[0], w_half(0, 0)) + dot(routed_b[1], w_half(0, 1)))

    locals_[3].wait()
    for h in range(2):
        def correct(t, _, h=h):
            columns = pl.ds(pl.multiple_of(t * 256, 256), 256)
            x = rcv[h, :, :, columns].reshape(ROWS_A, 256)
            total = dot(x, hid[0:ROWS_A, :], ((0,), (0,)))
            total = total + dot(routed_b[h, :, columns], hid[ROWS_A:SLOTS, :], ((0,), (0,)))
            rows = pl.ds(pl.multiple_of(h * HALF_D + t * 256, 256), 256)
            total = total + res[rows, :].astype(F32)
            corr[rows, :] = total
            for b in range(2):
                top = jnp.max(jnp.abs(total[b * BLOCK : (b + 1) * BLOCK]), axis=0, keepdims=True)
                maxima[y, pl.ds(h * 14 + t * 2 + b, 1), :] = top
            return 0

        lax.fori_loop(0, 7, correct, 0)

    def max_copy(i):
        return pltpu.make_async_remote_copy(
            src_ref=maxima.at[y],
            dst_ref=maxima.at[y],
            send_sem=m_send.at[i],
            recv_sem=m_recv.at[i],
            device_id={"replica": (right, left, opposite)[i]},
            device_id_type=MESH,
        )

    for i in range(3):
        max_copy(i).start()
    for i in range(3):
        max_copy(i).wait()
    largest = jnp.maximum(jnp.maximum(maxima[0], maxima[1]), jnp.maximum(maxima[2], maxima[3]))
    scales_ref[...] = largest + 1e-6

    def code(b, _):
        rows = pl.ds(pl.multiple_of(b * BLOCK, BLOCK), BLOCK)
        res[rows, :] = (corr[rows, :] / scales_ref[pl.ds(b, 1), :]).astype(BF16)
        return 0

    lax.fori_loop(0, D // BLOCK, code, 0)

    weight_ready(1)
    weight_ready(2)

    def code_copy(i):
        peer = (right, left, opposite)[i]
        return pltpu.make_async_remote_copy(
            src_ref=res.at[pl.ds(pl.multiple_of(peer * SHARD, SHARD), SHARD)],
            dst_ref=code_got.at[i],
            send_sem=c_send.at[i],
            recv_sem=c_recv.at[i],
            device_id={"replica": peer},
            device_id_type=MESH,
        )

    for i in range(3):
        code_copy(i).start()

    def partial(h, dst):
        def tile(t, _):
            rows = pl.ds(pl.multiple_of(t * 256, 256), 256)
            for q in range(2):
                s = 2 * h + q
                value = dot(gate_grad[rows, :], wf[1, s], ((1,), (1,))) + dot(
                    up_grad[rows, :], wf[2, s], ((1,), (1,))
                )
                dst[pl.ds(t * 16, 16), :, q * SHARD : (q + 1) * SHARD] = value.astype(BF16).reshape(
                    16, 16, SHARD
                )
            return 0

        lax.fori_loop(0, 2, tile, 0)

        def tile_b(t, _):
            rows = pl.ds(pl.multiple_of(ROWS_A + t * 128, 128), 128)
            values = []
            for q in range(2):
                s = 2 * h + q
                value = dot(gate_grad[rows, :], wf[1, s], ((1,), (1,))) + dot(
                    up_grad[rows, :], wf[2, s], ((1,), (1,))
                )
                values.append(value.reshape(16, 1, 8, SHARD))
            both = jnp.concatenate(values, axis=1).reshape(16, 16, SHARD)
            dst[pl.ds(t * 16, 16), :, HALF_D:WIDE] = both.astype(BF16)
            return 0

        lax.fori_loop(0, 2, tile_b, 0)

    partial(other, part_send)
    swap = pltpu.make_async_remote_copy(
        src_ref=part_send,
        dst_ref=part_got,
        send_sem=p_send,
        recv_sem=p_recv,
        device_id={"tensor": other},
        device_id_type=MESH,
    )
    swap.start()
    partial(core, part_own)

    def dispatched(i, _):
        dispatch(i).wait_send()
        return 0

    lax.fori_loop(1, EXPERTS, dispatched, 0)
    swap.wait()

    def give_back(i):
        peer = lax.rem(me + i, EXPERTS)
        return pltpu.make_async_remote_copy(
            src_ref=out.at[peer],
            dst_ref=ret.at[me],
            send_sem=r_send.at[i],
            recv_sem=r_recv.at[i],
            device_id={"expert": peer},
            device_id_type=MESH,
        )

    def summed(e):
        return (part_own[e].astype(F32) + part_got[e].astype(F32)).astype(BF16)

    def start_back(i, _):
        e = lax.rem(me + i, EXPERTS)
        out[e] = summed(e)
        give_back(i).start()
        return 0

    lax.fori_loop(1, EXPERTS, start_back, 0)
    ret[me] = summed(me)

    for i in range(3):
        code_copy(i).wait()

    def add_codes(t, _):
        rows = pl.ds(pl.multiple_of(t * 128, 128), 128)
        total = res[pl.ds(pl.multiple_of(y * SHARD + t * 128, 128), 128), :].astype(F32)
        for i in range(3):
            total = total + code_got[i, rows, :].astype(F32)
        sums_ref[rows, :] = total
        return 0

    lax.fori_loop(0, SHARD // 128, add_codes, 0)

    def came_back(i, _):
        give_back(i).wait()
        return 0

    lax.fori_loop(1, EXPERTS, came_back, 0)
    back_b = ret[:, :, HALF_D:WIDE].reshape(ROWS_A, SHARD)
    for q in range(2):
        columns = slice(q * SHARD, (q + 1) * SHARD)
        total = dot(pick_t[0], ret[:, :, columns].reshape(ROWS_A, SHARD)) + dot(pick_t[1 + q], back_b)
        grad_in_ref[:, columns] = total.astype(BF16)

    for w in range(3):
        for i in range(4):
            weight_copy(w, i).wait_send()
        for i in range(2):
            weight_relay(w, i).wait_send()


def local(grad_out, gates, expert_ids, gate_pre, up_pre, w_gate, w_up, w_down, residual):
    whole = pl.BlockSpec(memory_space=pltpu.VMEM)
    hbm = pl.BlockSpec(memory_space=pl.ANY)
    message = (EXPERTS, 16, WIDE)
    dma = pltpu.SemaphoreType.DMA
    grad_in, code_sums, scales = pl.pallas_call(
        kernel,
        out_shape=(
            jax.ShapeDtypeStruct((TOKENS, HALF_D), BF16),
            jax.ShapeDtypeStruct((SHARD, GROUP), F32),
            jax.ShapeDtypeStruct((D // BLOCK, GROUP), F32),
        ),
        in_specs=[whole, whole] + [hbm] * 7,
        out_specs=(whole, whole, whole),
        scratch_shapes=[
            pltpu.VMEM(message, BF16),
            pltpu.VMEM((2,) + message, BF16),
            pltpu.VMEM(message, BF16),
            pltpu.VMEM(message, BF16),
            pltpu.VMEM(message, BF16),
            pltpu.VMEM(message, BF16),
            pltpu.VMEM((3, REPLICAS, SHARD, GROUP), BF16),
            pltpu.VMEM((2, ROWS_B, HALF_D), BF16),
            pltpu.VMEM((3, ROWS_A, TOKENS), BF16),
            pltpu.VMEM((3, TOKENS, ROWS_A), BF16),
            pltpu.VMEM((TOKENS, HALF_D), BF16),
            pltpu.VMEM((SLOTS, GROUP), BF16),
            pltpu.VMEM((SLOTS, GROUP), BF16),
            pltpu.VMEM((SLOTS, GROUP), BF16),
            pltpu.VMEM((SLOTS, GROUP), F32),
            pltpu.VMEM((SLOTS, GROUP), F32),
            pltpu.VMEM((SLOTS, GROUP), BF16),
            pltpu.VMEM((SLOTS, GROUP), BF16),
            pltpu.VMEM((D, GROUP), BF16),
            pltpu.VMEM((D, GROUP), F32),
            pltpu.VMEM((3, SHARD, GROUP), BF16),
            pltpu.VMEM((REPLICAS, D // BLOCK, GROUP), F32),
            dma((EXPERTS,)),
            dma((EXPERTS,)),
            dma((EXPERTS,)),
            dma((EXPERTS,)),
            dma((EXPERTS,)),
            dma((EXPERTS,)),
            dma((18,)),
            dma((18,)),
            dma,
            dma,
            dma((3,)),
            dma((3,)),
            dma((3,)),
            dma((3,)),
            dma((8,)),
        ],
        compiler_params=pltpu.CompilerParams(
            collective_id=0, has_side_effects=True, vmem_limit_bytes=62 * 2**20
        ),
        cost_estimate=pl.CostEstimate(flops=11_300_000_000, bytes_accessed=14_000_000, transcendentals=400_000),
    )(
        expert_ids.T, gates.T, grad_out, gate_pre[0], up_pre[0], w_gate[0], w_up[0], w_down[0], residual[0]
    )
    return grad_in, code_sums[None], scales[None]


def solution(mesh):
    spec = P("expert", "replica", "tensor")
    tokens = P(("expert", "replica"), None)
    in_specs = (tokens,) * 3 + (spec,) * 6
    out_specs = (P(("expert", "replica"), "tensor"), spec, P("expert", None, "tensor"))
    return jax.shard_map(local, mesh=mesh, in_specs=in_specs, out_specs=out_specs, check_vma=False)
```

time: 482 us -> 191 us (0.40)
  waiting for transfers between devices: 210 us -> 0 us
  Pallas kernels: 0 us -> 184 us
  local copies, waits for them, and re-layouts: 117 us -> 6.21 us
  other arithmetic: 45.6 us -> 0 us
  blocking collectives: 38.6 us -> 0 us
  matrix products: 32 us -> 0 us
  starting transfers between devices: 20.4 us -> 0 us
  between operations: 14.2 us -> 0.64 us
    pallas_call x0 -> x1, Pallas kernels: none -> 184 us  [local(): pl.pallas_call(kernel, out_shape=(jax.ShapeDtypeStruct((TOKENS, HALF_D),...]
    all_to_all x2 -> x0, waiting for transfers between devices: 147 us -> none  [the longest x1 107 us: local(): lax.all_to_all(outgoing.reshape(expert_count, capacity, model_width), 'ex...]
    unnamed x12 -> x3, local copies, waits for them, and re-layouts: 56.5 us -> 6.21 us
    reduce_scatter x1 -> x0, waiting for transfers between devices: 46.6 us -> none  [local(): lax.psum_scatter(codes.astype(jnp.bfloat16), 'replica', scatter_dimension...]
    dot_general x4 -> x0, matrix products: 32 us -> none  [the longest x2 16.6 us: contract_rows(): lax.dot_general(left, right, (((1,), (1,)), ((), ())), preferred_element_...]
    reduce_sum x3 -> x0, other arithmetic: 25.4 us -> none  [the longest x1 20.8 us: local(): returned = jnp.sum(arrived.astype(jnp.float32), axis=2).astype(jnp.bfloat16)]
    all_to_all x1 -> x0, blocking collectives: 23.5 us -> none  [local(): lax.all_to_all(lax.all_to_all(stacked, 'expert', split_axis=0, concat_axi...]
    all_to_all x1 -> x0, local copies, waits for them, and re-layouts: 22.9 us -> none  [local(): lax.all_to_all(stacked, 'expert', split_axis=0, concat_axis=0, tiled=True)]
  transfers between devices with their start and end apart: 6 -> 0, of which waited for: 4 -> 0; matrix products, arithmetic and copies ran while one was open for 13% -> 0% of each run, Pallas kernels for 0% -> 0%
where the time goes in v1:
time: 191 us; the launch traced here: 190 us
  Pallas kernels  184 us (96%)
  local copies, waits for them, and re-layouts  6.21 us (3%)
    pallas_call x1, Pallas kernels, local(): pl.pallas_call(kernel, out_shape=(jax.ShapeDtypeStruct((TOKENS, HALF_D),...  184 us
    unnamed x3, local copies, waits for them, and re-layouts  6.21 us

profile of v1, /device:TPU:1, one launch (start us, length us, event | category | flops | bytes accessed | tf_op | source)
XLA Modules:
  0.0 190.5 jit_solution(3689620181318891093)
XLA Ops:
  0.6 183.6 %shard_map.112 = (bf16[128,1792]{1,0:T(8,128)(2,1)}, f32[896,512]{1,0:T(8,128)}, f32[28,512]{1,0:T(8,128)}) custom-call(s32[4,128]{1,0:T(4,128)} %bitcast.18, f32[4,128]{1,0:T(4,128)} %bitcast.19, bf16[128,3584]{1,0:T(8,128)(2,1)} %grad_hbm.1, bf16[768,512]{1,0:T(8,128)(2,1)} %bitcast.16, bf16[768,512]{1,0:T(8,128)(2,1)} %bitcast.17, ...), custom_call_target="tpu_custom_call" | custom-call | flops 11299999744 | bytes 14000000 | tf_op jit(solution)/shard_map/pallas_call | solution.py:433
  184.3 1.5 copy.12
  185.8 1.8 copy.15
  187.6 2.9 %copy.16 = f32[1,896,512]{2,1,0:T(8,128)} copy(f32[1,896,512]{2,1,0:T(8,128)} %bitcast.10) | data formatting | bytes 3670016

commit v2 on v1

v2 whole, which is shorter than its diff:
```python
import jax
import jax.numpy as jnp
from jax import lax
from jax.experimental import pallas as pl
from jax.experimental.pallas import tpu as pltpu
from jax.sharding import PartitionSpec as P

MESH = pl.DeviceIdType.MESH
BF16, F32 = jnp.bfloat16, jnp.float32

EXPERTS, REPLICAS = 32, 4
TOKENS, TOP, CAP = 128, 4, 24
D, GROUP, SHARD, BLOCK = 3584, 512, 896, 128
HALF_D = D // 2
ROWS_A, ROWS_B = EXPERTS * 16, EXPERTS * 8
SLOTS = ROWS_A + ROWS_B
WIDE = 3 * SHARD
CUT = SHARD // 2
TILE = 8 * CAP


def dot(a, b, dims=((1,), (0,))):
    return lax.dot_general(a, b, (dims, ((), ())), preferred_element_type=F32)


def kernel(
    ids_ref, gates_ref, grad_hbm, gate_hbm, up_hbm, wg_hbm, wu_hbm, wd_hbm, res_hbm,
    grad_in_ref, sums_ref, scales_ref,
    out, rcv, ret, part, part_got, wf, routed, pick, pick_t, grad, gate_pre, up_pre,
    hid, fac_gate, fac_up, gate_grad, up_grad, res, corr, code_got, maxima, total_in,
    a_send, a_recv, f_send, f_recv, r_send, r_recv, w_send, w_recv, p_send, p_recv,
    m_send, m_recv, c_send, c_recv, l_sem,
):
    me = lax.axis_index("expert")
    y = lax.axis_index("replica")
    core = lax.axis_index("tensor")
    other = 1 - core
    odd = lax.rem(y, 2)
    near = lax.div(y, 2)
    pair = y + 1 - 2 * odd
    next_ = lax.rem(y + 3 + 2 * odd, REPLICAS)
    opposite = lax.rem(y + 2, REPLICAS)
    weights = (wd_hbm, wg_hbm, wu_hbm)

    def saved(s):
        source = lax.rem(me + EXPERTS - s, EXPERTS)
        return (
            pltpu.make_async_copy(gate_hbm.at[source], gate_pre.at[s], l_sem.at[1]),
            pltpu.make_async_copy(up_hbm.at[source], up_pre.at[s], l_sem.at[2]),
        )

    grad_copy = pltpu.make_async_copy(
        grad_hbm.at[:, pl.ds(pl.multiple_of(core * HALF_D, HALF_D), HALF_D)], grad, l_sem.at[0]
    )
    res_copy = pltpu.make_async_copy(res_hbm, res, l_sem.at[3])
    own_weights = [pltpu.make_async_copy(weights[w], wf.at[w, y], l_sem.at[4 + w]) for w in range(3)]
    grad_copy.start()

    barrier = pltpu.get_barrier_semaphore()

    def greet(i, _):
        pl.semaphore_signal(
            barrier, inc=1, device_id={"expert": lax.rem(me + i, EXPERTS)}, device_id_type=MESH
        )
        return 0

    for peer in (pair, next_, opposite):
        pl.semaphore_signal(barrier, inc=1, device_id={"replica": peer}, device_id_type=MESH)
    pl.semaphore_signal(barrier, inc=1, device_id={"tensor": other}, device_id_type=MESH)
    lax.fori_loop(1, EXPERTS, greet, 0)

    def start_saved(s, _):
        for copy in saved(s):
            copy.start()
        return 0

    lax.fori_loop(0, EXPERTS, start_saved, 0)
    for copy in own_weights:
        copy.start()
    res_copy.start()

    ids = ids_ref[...].astype(F32)
    expert_row = lax.broadcasted_iota(jnp.int32, (EXPERTS, TOKENS), 0).astype(F32)
    named = jnp.zeros((EXPERTS, TOKENS), F32)
    for k in range(TOP):
        named = named + jnp.where(ids[k : k + 1, :] == expert_row, 1.0, 0.0)
    before = jnp.where(
        lax.broadcasted_iota(jnp.int32, (TOKENS, TOKENS), 0)
        < lax.broadcasted_iota(jnp.int32, (TOKENS, TOKENS), 1),
        1.0,
        0.0,
    ).astype(BF16)
    earlier = dot(named.astype(BF16), before)
    keys = []
    for k in range(TOP):
        id_k = ids[k : k + 1, :]
        slot_k = jnp.sum(jnp.where(id_k == expert_row, earlier, 0.0), axis=0, keepdims=True)
        keys.append(id_k * 32.0 + slot_k)
    row = lax.broadcasted_iota(jnp.int32, (ROWS_A, 1), 0)
    in_row = jnp.bitwise_and(row, 15)
    base = jnp.bitwise_and(me + jnp.right_shift(row, 4), EXPERTS - 1) * 32
    key_a = (base + in_row).astype(F32)
    key_b = (base + 16 + jnp.bitwise_and(row, 7)).astype(F32)
    lower = in_row < 8
    hot = jnp.zeros((ROWS_A, TOKENS), F32)
    weigh = jnp.zeros((ROWS_A, TOKENS), F32)
    hot_b = jnp.zeros((ROWS_A, TOKENS), F32)
    weigh_b = jnp.zeros((ROWS_A, TOKENS), F32)
    for k in range(TOP):
        same = key_a == keys[k]
        same_b = key_b == keys[k]
        gate_k = gates_ref[k : k + 1, :]
        hot = hot + jnp.where(same, 1.0, 0.0)
        weigh = weigh + jnp.where(same, gate_k, 0.0)
        hot_b = hot_b + jnp.where(same_b, 1.0, 0.0)
        weigh_b = weigh_b + jnp.where(same_b, gate_k, 0.0)
    gate_a = jnp.sum(weigh, axis=1, keepdims=True)
    gate_b = jnp.sum(weigh_b, axis=1, keepdims=True)
    pick[0] = hot.astype(BF16)
    pick[1] = jnp.where(lower, hot_b, 0.0).astype(BF16)
    pick[2] = jnp.where(lower, 0.0, hot_b).astype(BF16)

    def weight_copy(number):
        if number < 12:
            w, lo = number % 6 // 2, number % 2 * CUT
            owner, peer = y, (pair if number < 6 else next_)
            src = weights[w].at[pl.ds(lo, CUT)]
        else:
            w, lo = ((0, 0), (0, CUT), (2, 0), (1, 0), (1, CUT), (2, CUT))[number - 12]
            owner, peer = (pair, next_) if number < 15 else (next_, pair)
            src = wf.at[w, owner, pl.ds(lo, CUT)]
        return pltpu.make_async_remote_copy(
            src_ref=src,
            dst_ref=wf.at[w, owner, pl.ds(lo, CUT)],
            send_sem=w_send.at[number],
            recv_sem=w_recv.at[number],
            device_id={"replica": peer},
            device_id_type=MESH,
        )

    def weights_start(*numbers):
        for number in numbers:
            weight_copy(number).start()

    def weights_wait(*numbers):
        for number in numbers:
            weight_copy(number).wait_recv()

    pl.semaphore_wait(barrier, EXPERTS + 3)
    weights_start(0, 6, 1, 7, 2, 3, 4, 5)

    def dispatch(s):
        return pltpu.make_async_remote_copy(
            src_ref=out.at[s],
            dst_ref=rcv.at[core, s],
            send_sem=a_send.at[s],
            recv_sem=a_recv.at[s],
            device_id={"expert": lax.rem(me + s, EXPERTS)},
            device_id_type=MESH,
        )

    def start_dispatch(s, _):
        dispatch(s).start()
        return 0

    grad_copy.wait()
    own = pltpu.make_async_copy(out.at[0], rcv.at[core, 0], l_sem.at[7])
    for q in range(4):
        rows = pl.ds(q * 128, 128)
        block = dot(pick[0, rows, :], grad[...]) * gate_a[q * 128 : (q + 1) * 128]
        out[pl.ds(q * 8, 8), :, 0:HALF_D] = block.astype(BF16).reshape(8, 16, HALF_D)
        block = dot(pick[1, rows, :], grad[:, 0:SHARD]) + dot(pick[2, rows, :], grad[:, SHARD:HALF_D])
        block = block * gate_b[q * 128 : (q + 1) * 128]
        out[pl.ds(q * 8, 8), :, HALF_D:WIDE] = block.astype(BF16).reshape(8, 16, SHARD)
        lax.fori_loop(max(1, q * 8), q * 8 + 8, start_dispatch, 0)
        if q == 0:
            own.start()

    def share(s):
        return pltpu.make_async_remote_copy(
            src_ref=rcv.at[core, s],
            dst_ref=rcv.at[core, s],
            send_sem=f_send.at[s],
            recv_sem=f_recv.at[s],
            device_id={"tensor": other},
            device_id_type=MESH,
        )

    def pass_on(s, _):
        dispatch(s).wait_recv()
        share(s).start()
        return 0

    def share_got(s, _):
        share(s).wait()
        return 0

    own.wait()
    share(0).start()

    pltpu.make_async_copy(gate_hbm, gate_pre, l_sem.at[1]).wait()
    pltpu.make_async_copy(up_hbm, up_pre, l_sem.at[2]).wait()

    def activate(g, _):
        a = gate_pre[pl.ds(g * 8, 8)].astype(F32)
        u = up_pre[pl.ds(g * 8, 8)].astype(F32)
        for lo, hi, at in ((0, 16, g * TILE), (16, 24, g * TILE + 128)):
            n = 8 * (hi - lo)
            a_part = a[:, lo:hi].reshape(n, GROUP)
            u_part = u[:, lo:hi].reshape(n, GROUP)
            sigma = 1.0 / (1.0 + jnp.exp(-a_part))
            silu = a_part * sigma
            to = pl.ds(pl.multiple_of(at, 64), n)
            hid[to, :] = (silu * u_part).astype(BF16)
            fac_up[to, :] = silu
            fac_gate[to, :] = u_part * sigma * (1.0 + a_part * (1.0 - sigma))
        return 0

    lax.fori_loop(0, 4, activate, 0)

    def tile_of(g):
        return pl.ds(pl.multiple_of(g * TILE, TILE), TILE)

    def unfold(g):
        lax.fori_loop(g * 8, g * 8 + 8, share_got, 0)
        for h in range(2):
            routed[h, g * TILE : g * TILE + 128, :] = rcv[h, g * 8 : g * 8 + 8, :, 0:HALF_D].reshape(128, HALF_D)
            raw = rcv[h, g * 8 : g * 8 + 8, :, HALF_D:WIDE].astype(F32).reshape(8, 2, 8, SHARD)
            for q in range(2):
                routed[h, g * TILE + 128 : (g + 1) * TILE, q * SHARD : (q + 1) * SHARD] = (
                    raw[:, q].reshape(64, SHARD).astype(BF16)
                )

    def w_half(w, h):
        return wf[w, pl.ds(2 * h, 2)].reshape(HALF_D, GROUP)

    def hidden_grads(g, _):
        rows = tile_of(g)
        total = dot(routed[0, rows, :], w_half(0, 0)) + dot(routed[1, rows, :], w_half(0, 1))
        gate_grad[rows, :] = (total * fac_gate[rows, :]).astype(BF16)
        up_grad[rows, :] = (total * fac_up[rows, :]).astype(BF16)
        return 0

    def correct(lo, hi, first, last):
        for h in range(2):
            def step(t, _, h=h):
                columns = pl.ds(pl.multiple_of(t * 256, 256), 256)
                rows = pl.ds(pl.multiple_of(h * HALF_D + t * 256, 256), 256)
                total = dot(routed[h, lo:hi, columns], hid[lo:hi, :], ((0,), (0,)))
                total = total + (res[rows, :].astype(F32) if first else corr[rows, :])
                corr[rows, :] = total
                if last:
                    for b in range(2):
                        top = jnp.max(jnp.abs(total[b * BLOCK : (b + 1) * BLOCK]), axis=0, keepdims=True)
                        maxima[y, pl.ds(h * 14 + t * 2 + b, 1), :] = top
                return 0

            lax.fori_loop(0, 7, step, 0)

    def swap(stage, g):
        block = pl.ds(g * 8, 8)
        return pltpu.make_async_remote_copy(
            src_ref=part.at[stage, block],
            dst_ref=part_got.at[block],
            send_sem=p_send.at[g],
            recv_sem=p_recv.at[g],
            device_id={"tensor": other},
            device_id_type=MESH,
        )

    def partial(stage):
        half = near if stage == 0 else 1 - near

        def group(g, _):
            rows = tile_of(g)
            values = []
            for q in range(2):
                s = 2 * half + q
                value = dot(gate_grad[rows, :], wf[1, s], ((1,), (1,))) + dot(
                    up_grad[rows, :], wf[2, s], ((1,), (1,))
                )
                part[stage, pl.ds(g * 8, 8), :, q * SHARD : (q + 1) * SHARD] = (
                    value[0:128].astype(BF16).reshape(8, 16, SHARD)
                )
                values.append(value[128:TILE].reshape(8, 1, 8, SHARD))
            both = jnp.concatenate(values, axis=1).reshape(8, 16, SHARD)
            part[stage, pl.ds(g * 8, 8), :, HALF_D:WIDE] = both.astype(BF16)

            @pl.when(half != core)
            def _():
                swap(stage, g).start()

            return 0

        return group

    def give_back(s):
        return pltpu.make_async_remote_copy(
            src_ref=out.at[s],
            dst_ref=ret.at[s],
            send_sem=r_send.at[s],
            recv_sem=r_recv.at[s],
            device_id={"expert": lax.rem(me + EXPERTS - s, EXPERTS)},
            device_id_type=MESH,
        )

    def send_back(stage, lo, hi):
        half = near if stage == 0 else 1 - near

        def summed(s):
            return (part[stage, s].astype(F32) + part_got[s].astype(F32)).astype(BF16)

        def one(s, _):
            dispatch(s).wait_send()
            out[s] = summed(s)
            give_back(s).start()
            return 0

        @pl.when(half == core)
        def _():
            for g in range(lo, hi):
                swap(stage, g).wait_recv()
                if g == 0:
                    ret[0] = summed(0)
                lax.fori_loop(max(1, g * 8), g * 8 + 8, one, 0)

    lax.fori_loop(1, 3, pass_on, 0)
    weights_wait(0)
    weights_start(12)
    lax.fori_loop(3, 6, pass_on, 0)
    weights_wait(1)
    weights_start(13, 8, 9, 11, 10)
    for j in range(3):
        pick_t[j] = jnp.transpose(pick[j].astype(F32)).astype(BF16)
    lax.fori_loop(6, 8, pass_on, 0)
    unfold(0)
    lax.fori_loop(8, 16, pass_on, 0)
    unfold(1)
    own_weights[0].wait()
    weights_wait(6, 7, 12, 13)
    lax.fori_loop(0, 2, hidden_grads, 0)
    lax.fori_loop(16, 24, pass_on, 0)
    unfold(2)
    hidden_grads(2, 0)
    res_copy.wait()
    correct(0, 3 * TILE, True, False)
    weights_wait(8, 4)
    weights_start(15, 14)
    lax.fori_loop(24, EXPERTS, pass_on, 0)
    weights_wait(9)
    weights_start(16)
    own_weights[1].wait()
    own_weights[2].wait()
    weights_wait(2, 3, 5)
    lax.fori_loop(0, 3, partial(0), 0)
    unfold(3)
    hidden_grads(3, 0)
    partial(0)(3, 0)
    send_back(0, 0, 4)

    correct(3 * TILE, SLOTS, False, True)

    def max_copy(i):
        return pltpu.make_async_remote_copy(
            src_ref=maxima.at[y],
            dst_ref=maxima.at[y],
            send_sem=m_send.at[i],
            recv_sem=m_recv.at[i],
            device_id={"replica": (opposite, pair, next_)[i]},
            device_id_type=MESH,
        )

    for i in range(3):
        max_copy(i).start()
    weights_wait(11)
    weights_start(17)
    for i in range(3):
        max_copy(i).wait()
    largest = jnp.maximum(jnp.maximum(maxima[0], maxima[1]), jnp.maximum(maxima[2], maxima[3]))
    scales_ref[...] = largest + 1e-6

    def code(b, _):
        rows = pl.ds(pl.multiple_of(b * BLOCK, BLOCK), BLOCK)
        res[rows, :] = (corr[rows, :] / scales_ref[pl.ds(b, 1), :]).astype(BF16)
        return 0

    lax.fori_loop(0, D // BLOCK, code, 0)

    def code_copy(i):
        peer = (opposite, pair, next_)[i]
        return pltpu.make_async_remote_copy(
            src_ref=res.at[pl.ds(pl.multiple_of(peer * SHARD, SHARD), SHARD)],
            dst_ref=code_got.at[i],
            send_sem=c_send.at[i],
            recv_sem=c_recv.at[i],
            device_id={"replica": peer},
            device_id_type=MESH,
        )

    for i in range(3):
        code_copy(i).start()

    weights_wait(10, 14, 15, 16, 17)
    lax.fori_loop(0, 4, partial(1), 0)
    send_back(1, 0, 4)

    def came_back(s, _):
        give_back(s).wait()
        return 0

    def combine(g):
        rows = slice(g * 128, (g + 1) * 128)
        back_b = ret[g * 8 : g * 8 + 8, :, HALF_D:WIDE].reshape(128, SHARD)
        for q in range(2):
            columns = slice(q * SHARD, (q + 1) * SHARD)
            total = dot(pick_t[0, :, rows], ret[g * 8 : g * 8 + 8, :, columns].reshape(128, SHARD))
            total = total + dot(pick_t[1 + q, :, rows], back_b)
            if g > 0:
                total = total + total_in[:, columns]
            if g < 3:
                total_in[:, columns] = total
            else:
                grad_in_ref[:, columns] = total.astype(BF16)

    for g in range(3):
        lax.fori_loop(max(1, g * 8), g * 8 + 8, came_back, 0)
        combine(g)

    for i in range(3):
        code_copy(i).wait()

    def add_codes(t, _):
        rows = pl.ds(pl.multiple_of(t * 128, 128), 128)
        total = res[pl.ds(pl.multiple_of(y * SHARD + t * 128, 128), 128), :].astype(F32)
        for i in range(3):
            total = total + code_got[i, rows, :].astype(F32)
        sums_ref[rows, :] = total
        return 0

    lax.fori_loop(0, SHARD // 128, add_codes, 0)
    lax.fori_loop(24, EXPERTS, came_back, 0)
    combine(3)

    for number in range(18):
        weight_copy(number).wait_send()
    for stage, half in ((0, near), (1, 1 - near)):
        @pl.when(half != core)
        def _(stage=stage):
            for g in range(4):
                swap(stage, g).wait_send()


def local(grad_out, gates, expert_ids, gate_pre, up_pre, w_gate, w_up, w_down, residual):
    whole = pl.BlockSpec(memory_space=pltpu.VMEM)
    hbm = pl.BlockSpec(memory_space=pl.ANY)
    message = (EXPERTS, 16, WIDE)
    dma = pltpu.SemaphoreType.DMA
    saved = [a.reshape(EXPERTS, CAP, GROUP) for a in (gate_pre, up_pre)]
    grad_in, code_sums, scales = pl.pallas_call(
        kernel,
        out_shape=(
            jax.ShapeDtypeStruct((TOKENS, HALF_D), BF16),
            jax.ShapeDtypeStruct((SHARD, GROUP), F32),
            jax.ShapeDtypeStruct((D // BLOCK, GROUP), F32),
        ),
        in_specs=[whole, whole] + [hbm] * 7,
        out_specs=(whole, whole, whole),
        scratch_shapes=[
            pltpu.VMEM(message, BF16),
            pltpu.VMEM((2,) + message, BF16),
            pltpu.VMEM(message, BF16),
            pltpu.VMEM((2,) + message, BF16),
            pltpu.VMEM(message, BF16),
            pltpu.VMEM((3, REPLICAS, SHARD, GROUP), BF16),
            pltpu.VMEM((2, SLOTS, HALF_D), BF16),
            pltpu.VMEM((3, ROWS_A, TOKENS), BF16),
            pltpu.VMEM((3, TOKENS, ROWS_A), BF16),
            pltpu.VMEM((TOKENS, HALF_D), BF16),
            pltpu.VMEM((EXPERTS, CAP, GROUP), BF16),
            pltpu.VMEM((EXPERTS, CAP, GROUP), BF16),
            pltpu.VMEM((SLOTS, GROUP), BF16),
            pltpu.VMEM((SLOTS, GROUP), F32),
            pltpu.VMEM((SLOTS, GROUP), F32),
            pltpu.VMEM((SLOTS, GROUP), BF16),
            pltpu.VMEM((SLOTS, GROUP), BF16),
            pltpu.VMEM((D, GROUP), BF16),
            pltpu.VMEM((D, GROUP), F32),
            pltpu.VMEM((3, SHARD, GROUP), BF16),
            pltpu.VMEM((REPLICAS, D // BLOCK, GROUP), F32),
            pltpu.VMEM((TOKENS, HALF_D), F32),
            dma((EXPERTS,)),
            dma((EXPERTS,)),
            dma((EXPERTS,)),
            dma((EXPERTS,)),
            dma((EXPERTS,)),
            dma((EXPERTS,)),
            dma((18,)),
            dma((18,)),
            dma((4,)),
            dma((4,)),
            dma((3,)),
            dma((3,)),
            dma((3,)),
            dma((3,)),
            dma((8,)),
        ],
        compiler_params=pltpu.CompilerParams(
            collective_id=0, has_side_effects=True, vmem_limit_bytes=62 * 2**20
        ),
        cost_estimate=pl.CostEstimate(flops=11_300_000_000, bytes_accessed=14_000_000, transcendentals=400_000),
    )(
        expert_ids.T, gates.T, grad_out, *saved, w_gate[0], w_up[0], w_down[0], residual[0]
    )
    return grad_in, code_sums[None], scales[None]


def solution(mesh):
    spec = P("expert", "replica", "tensor")
    tokens = P(("expert", "replica"), None)
    in_specs = (tokens,) * 3 + (spec,) * 6
    out_specs = (P(("expert", "replica"), "tensor"), spec, P("expert", None, "tensor"))
    return jax.shard_map(local, mesh=mesh, in_specs=in_specs, out_specs=out_specs, check_vma=False)
```

time: 191 us -> 158 us (0.83)
  Pallas kernels: 184 us -> 151 us
    pallas_call x1, Pallas kernels: 184 us -> 151 us  [local(): pl.pallas_call(kernel, out_shape=(jax.ShapeDtypeStruct((TOKENS, HALF_D),...]
where the time goes in v2:
time: 158 us
  Pallas kernels  151 us (96%)
  local copies, waits for them, and re-layouts  6.21 us (4%)
    pallas_call x1, Pallas kernels, local(): pl.pallas_call(kernel, out_shape=(jax.ShapeDtypeStruct((TOKENS, HALF_D),...  151 us
    unnamed x3, local copies, waits for them, and re-layouts  6.21 us

profile of v2, /device:TPU:1, one launch (start us, length us, event | category | flops | bytes accessed | tf_op | source)
XLA Modules:
  0.0 157.6 jit_solution(14420025607799552711)
XLA Ops:
  0.6 150.7 %shard_map.112 = (bf16[128,1792]{1,0:T(8,128)(2,1)}, f32[896,512]{1,0:T(8,128)}, f32[28,512]{1,0:T(8,128)}) custom-call(s32[4,128]{1,0:T(4,128)} %bitcast.18, f32[4,128]{1,0:T(4,128)} %bitcast.19, bf16[128,3584]{1,0:T(8,128)(2,1)} %grad_hbm.1, bf16[32,24,512]{2,1,0:T(8,128)(2,1)} %bitcast.16, bf16[32,24,512]{2,1,0:T(8,128)(2,1)} %bitcast.17, ...), custom_call_target="tpu_custom_call" | custom-call | flops 11299999744 | bytes 14000000 | tf_op jit(solution)/shard_map/pallas_call | solution.py:459
  151.4 1.5 copy.12
  152.9 1.8 %copy.15 = bf16[128,1792]{1,0:T(8,128)(2,1)} copy(bf16[128,1792]{1,0:T(8,128)(2,1)} %get-tuple-element.15) | data formatting | bytes 917504
  154.7 2.9 %copy.16 = f32[1,896,512]{2,1,0:T(8,128)} copy(f32[1,896,512]{2,1,0:T(8,128)} %bitcast.10) | data formatting | bytes 3670016

commit v3 on v2

--- a/solution.py
+++ b/solution.py
@@ -27,7 +27,7 @@
     ids_ref, gates_ref, grad_hbm, gate_hbm, up_hbm, wg_hbm, wu_hbm, wd_hbm, res_hbm,
     grad_in_ref, sums_ref, scales_ref,
     out, rcv, ret, part, part_got, wf, routed, pick, pick_t, grad, gate_pre, up_pre,
-    hid, fac_gate, fac_up, gate_grad, up_grad, res, corr, code_got, maxima, total_in,
+    hid, fac_gate, fac_up, gate_grad, up_grad, res, corr, code_got, code_sum, maxima, total_in,
     a_send, a_recv, f_send, f_recv, r_send, r_recv, w_send, w_recv, p_send, p_recv,
     m_send, m_recv, c_send, c_recv, l_sem,
 ):
@@ -42,19 +42,17 @@
     opposite = lax.rem(y + 2, REPLICAS)
     weights = (wd_hbm, wg_hbm, wu_hbm)
 
-    def saved(s):
-        source = lax.rem(me + EXPERTS - s, EXPERTS)
-        return (
-            pltpu.make_async_copy(gate_hbm.at[source], gate_pre.at[s], l_sem.at[1]),
-            pltpu.make_async_copy(up_hbm.at[source], up_pre.at[s], l_sem.at[2]),
-        )
-
     grad_copy = pltpu.make_async_copy(
         grad_hbm.at[:, pl.ds(pl.multiple_of(core * HALF_D, HALF_D), HALF_D)], grad, l_sem.at[0]
     )
     res_copy = pltpu.make_async_copy(res_hbm, res, l_sem.at[3])
     own_weights = [pltpu.make_async_copy(weights[w], wf.at[w, y], l_sem.at[4 + w]) for w in range(3)]
-    grad_copy.start()
+    saved = [
+        pltpu.make_async_copy(gate_hbm, gate_pre, l_sem.at[1]),
+        pltpu.make_async_copy(up_hbm, up_pre, l_sem.at[2]),
+    ]
+    for copy in [grad_copy] + saved + own_weights + [res_copy]:
+        copy.start()
 
     barrier = pltpu.get_barrier_semaphore()
 
@@ -68,16 +66,6 @@
         pl.semaphore_signal(barrier, inc=1, device_id={"replica": peer}, device_id_type=MESH)
     pl.semaphore_signal(barrier, inc=1, device_id={"tensor": other}, device_id_type=MESH)
     lax.fori_loop(1, EXPERTS, greet, 0)
-
-    def start_saved(s, _):
-        for copy in saved(s):
-            copy.start()
-        return 0
-
-    lax.fori_loop(0, EXPERTS, start_saved, 0)
-    for copy in own_weights:
-        copy.start()
-    res_copy.start()
 
     ids = ids_ref[...].astype(F32)
     expert_row = lax.broadcasted_iota(jnp.int32, (EXPERTS, TOKENS), 0).astype(F32)
@@ -198,25 +186,29 @@
     own.wait()
     share(0).start()
 
-    pltpu.make_async_copy(gate_hbm, gate_pre, l_sem.at[1]).wait()
-    pltpu.make_async_copy(up_hbm, up_pre, l_sem.at[2]).wait()
-
-    def activate(g, _):
-        a = gate_pre[pl.ds(g * 8, 8)].astype(F32)
-        u = up_pre[pl.ds(g * 8, 8)].astype(F32)
-        for lo, hi, at in ((0, 16, g * TILE), (16, 24, g * TILE + 128)):
-            n = 8 * (hi - lo)
-            a_part = a[:, lo:hi].reshape(n, GROUP)
-            u_part = u[:, lo:hi].reshape(n, GROUP)
+    for copy in saved:
+        copy.wait()
+
+    def activate(j, _):
+        a, u = [], []
+        for s in (2 * j, 2 * j + 1):
+            source = lax.rem(me + EXPERTS - s, EXPERTS)
+            a.append(gate_pre[source].astype(F32))
+            u.append(up_pre[source].astype(F32))
+        first = lax.div(j, 4) * TILE
+        step = lax.rem(j, 4)
+        for lo, hi, at in ((0, 16, first + step * 32), (16, 24, first + 128 + step * 16)):
+            a_part = jnp.concatenate([v[lo:hi] for v in a], axis=0)
+            u_part = jnp.concatenate([v[lo:hi] for v in u], axis=0)
             sigma = 1.0 / (1.0 + jnp.exp(-a_part))
             silu = a_part * sigma
-            to = pl.ds(pl.multiple_of(at, 64), n)
+            to = pl.ds(pl.multiple_of(at, 16), 2 * (hi - lo))
             hid[to, :] = (silu * u_part).astype(BF16)
             fac_up[to, :] = silu
             fac_gate[to, :] = u_part * sigma * (1.0 + a_part * (1.0 - sigma))
         return 0
 
-    lax.fori_loop(0, 4, activate, 0)
+    lax.fori_loop(0, EXPERTS // 2, activate, 0)
 
     def tile_of(g):
         return pl.ds(pl.multiple_of(g * TILE, TILE), TILE)
@@ -339,26 +331,30 @@
     own_weights[0].wait()
     weights_wait(6, 7, 12, 13)
     lax.fori_loop(0, 2, hidden_grads, 0)
+    res_copy.wait()
+    correct(0, 2 * TILE, True, False)
     lax.fori_loop(16, 24, pass_on, 0)
     unfold(2)
     hidden_grads(2, 0)
-    res_copy.wait()
-    correct(0, 3 * TILE, True, False)
     weights_wait(8, 4)
     weights_start(15, 14)
-    lax.fori_loop(24, EXPERTS, pass_on, 0)
-    weights_wait(9)
-    weights_start(16)
+    lax.fori_loop(24, 28, pass_on, 0)
     own_weights[1].wait()
     own_weights[2].wait()
     weights_wait(2, 3, 5)
-    lax.fori_loop(0, 3, partial(0), 0)
+    lax.fori_loop(0, 2, partial(0), 0)
+    lax.fori_loop(28, EXPERTS, pass_on, 0)
+    partial(0)(2, 0)
+    weights_wait(9)
+    weights_start(16)
+    send_back(0, 0, 3)
     unfold(3)
     hidden_grads(3, 0)
     partial(0)(3, 0)
-    send_back(0, 0, 4)
-
-    correct(3 * TILE, SLOTS, False, True)
+    send_back(0, 3, 4)
+    weights_wait(11)
+    weights_start(17)
+    correct(2 * TILE, SLOTS, False, True)
 
     def max_copy(i):
         return pltpu.make_async_remote_copy(
@@ -372,8 +368,6 @@
 
     for i in range(3):
         max_copy(i).start()
-    weights_wait(11)
-    weights_start(17)
     for i in range(3):
         max_copy(i).wait()
     largest = jnp.maximum(jnp.maximum(maxima[0], maxima[1]), jnp.maximum(maxima[2], maxima[3]))
@@ -386,10 +380,16 @@
 
     lax.fori_loop(0, D // BLOCK, code, 0)
 
+    def code_rows(owner, lo):
+        return pl.ds(pl.multiple_of(owner * SHARD + lo, CUT), CUT)
+
     def code_copy(i):
-        peer = (opposite, pair, next_)[i]
-        return pltpu.make_async_remote_copy(
-            src_ref=res.at[pl.ds(pl.multiple_of(peer * SHARD, SHARD), SHARD)],
+        peer = (pair, next_, pair, next_, pair, next_)[i]
+        owner = (opposite, opposite, pair, next_, pair, next_)[i]
+        lo = (CUT, 0, CUT, 0, 0, CUT)[i]
+        src = res.at[code_rows(owner, lo)] if i < 4 else code_sum.at[i - 4]
+        return pltpu.make_async_remote_copy(
+            src_ref=src,
             dst_ref=code_got.at[i],
             send_sem=c_send.at[i],
             recv_sem=c_recv.at[i],
@@ -397,12 +397,20 @@
             device_id_type=MESH,
         )
 
-    for i in range(3):
+    for i in range(4):
         code_copy(i).start()
+
+    def code_pass(i):
+        code_copy(1 - i).wait_recv()
+        owner, lo = ((pair, 0), (next_, CUT))[i]
+        code_sum[i] = (res[code_rows(owner, lo), :].astype(F32) + code_got[1 - i].astype(F32)).astype(BF16)
+        code_copy(4 + i).start()
 
     weights_wait(10, 14, 15, 16, 17)
     lax.fori_loop(0, 4, partial(1), 0)
     send_back(1, 0, 4)
+    for i in range(2):
+        code_pass(i)
 
     def came_back(s, _):
         give_back(s).wait()
@@ -426,28 +434,44 @@
         lax.fori_loop(max(1, g * 8), g * 8 + 8, came_back, 0)
         combine(g)
 
-    for i in range(3):
-        code_copy(i).wait()
+    for i in range(2, 6):
+        code_copy(i).wait_recv()
 
     def add_codes(t, _):
-        rows = pl.ds(pl.multiple_of(t * 128, 128), 128)
-        total = res[pl.ds(pl.multiple_of(y * SHARD + t * 128, 128), 128), :].astype(F32)
-        for i in range(3):
-            total = total + code_got[i, rows, :].astype(F32)
-        sums_ref[rows, :] = total
-        return 0
-
-    lax.fori_loop(0, SHARD // 128, add_codes, 0)
+        rows = pl.ds(pl.multiple_of(t * 64, 64), 64)
+        for lo, first, second in ((0, 3, 4), (CUT, 2, 5)):
+            total = res[pl.ds(pl.multiple_of(y * SHARD + lo + t * 64, 64), 64), :].astype(F32)
+            for i in (first, second):
+                total = total + code_got[i, rows, :].astype(F32)
+            sums_ref[pl.ds(pl.multiple_of(lo + t * 64, 64), 64), :] = total
+        return 0
+
+    lax.fori_loop(0, CUT // 64, add_codes, 0)
     lax.fori_loop(24, EXPERTS, came_back, 0)
     combine(3)
 
     for number in range(18):
         weight_copy(number).wait_send()
+    for i in range(6):
+        code_copy(i).wait_send()
     for stage, half in ((0, near), (1, 1 - near)):
         @pl.when(half != core)
         def _(stage=stage):
             for g in range(4):
                 swap(stage, g).wait_send()
+
+
+def hand_out(grad_ref, sums_ref, scales_ref, grad_out, sums_out, scales_out, sem):
+    copies = [
+        pltpu.make_async_copy(grad_ref, grad_out, sem.at[0]),
+        pltpu.make_async_copy(sums_ref, sums_out, sem.at[1]),
+    ]
+    for copy in copies:
+        copy.start()
+    for b in range(D // BLOCK):
+        scales_out[b] = scales_ref[b : b + 1, :]
+    for copy in copies:
+        copy.wait()
 
 
 def local(grad_out, gates, expert_ids, gate_pre, up_pre, w_gate, w_up, w_down, residual):
@@ -485,7 +509,8 @@
             pltpu.VMEM((SLOTS, GROUP), BF16),
             pltpu.VMEM((D, GROUP), BF16),
             pltpu.VMEM((D, GROUP), F32),
-            pltpu.VMEM((3, SHARD, GROUP), BF16),
+            pltpu.VMEM((6, CUT, GROUP), BF16),
+            pltpu.VMEM((2, CUT, GROUP), BF16),
             pltpu.VMEM((REPLICAS, D // BLOCK, GROUP), F32),
             pltpu.VMEM((TOKENS, HALF_D), F32),
             dma((EXPERTS,)),
@@ -500,8 +525,8 @@
             dma((4,)),
             dma((3,)),
             dma((3,)),
-            dma((3,)),
-            dma((3,)),
+            dma((6,)),
+            dma((6,)),
             dma((8,)),
         ],
         compiler_params=pltpu.CompilerParams(
@@ -511,7 +536,18 @@
     )(
         expert_ids.T, gates.T, grad_out, *saved, w_gate[0], w_up[0], w_down[0], residual[0]
     )
-    return grad_in, code_sums[None], scales[None]
+    grad_in, code_sums, scales = pl.pallas_call(
+        hand_out,
+        out_shape=(
+            jax.ShapeDtypeStruct((TOKENS, HALF_D), BF16),
+            jax.ShapeDtypeStruct((SHARD, GROUP), F32),
+            jax.ShapeDtypeStruct((D // BLOCK, 1, GROUP), F32),
+        ),
+        in_specs=[whole] * 3,
+        out_specs=(hbm, hbm, whole),
+        scratch_shapes=[dma((2,))],
+    )(grad_in, code_sums, scales)
+    return grad_in, code_sums[None], scales.reshape(1, D // BLOCK, GROUP)
 
 
 def solution(mesh):

time: 158 us -> 152 us (0.962)
  local copies, waits for them, and re-layouts: 6.21 us -> 0 us
    unnamed x3 -> x0, local copies, waits for them, and re-layouts: 6.21 us -> none
    pallas_call x0 -> x1, Pallas kernels: none -> 3.59 us  [local(): pl.pallas_call(hand_out, out_shape=(jax.ShapeDtypeStruct((TOKENS, HALF_D)...]
    pallas_call x1, Pallas kernels: 151 us -> 147 us  [local(): pl.pallas_call(kernel, out_shape=(jax.ShapeDtypeStruct((TOKENS, HALF_D),...]
where the time goes in v3:
time: 152 us; the launch traced here: 151 us
  Pallas kernels  151 us (99%)
    pallas_call x1, Pallas kernels, local(): pl.pallas_call(kernel, out_shape=(jax.ShapeDtypeStruct((TOKENS, HALF_D),...  147 us
    pallas_call x1, Pallas kernels, local(): pl.pallas_call(hand_out, out_shape=(jax.ShapeDtypeStruct((TOKENS, HALF_D)...  3.59 us

profile of v3, /device:TPU:1, one launch (start us, length us, event | category | flops | bytes accessed | tf_op | source)
XLA Modules:
  0.0 151.4 jit_solution(16553961013240452077)
XLA Ops:
  0.6 147.2 %shard_map.112 = (bf16[128,1792]{1,0:T(8,128)(2,1)}, f32[896,512]{1,0:T(8,128)}, f32[28,512]{1,0:T(8,128)}) custom-call(s32[4,128]{1,0:T(4,128)} %bitcast.18, f32[4,128]{1,0:T(4,128)} %bitcast.19, bf16[128,3584]{1,0:T(8,128)(2,1)} %grad_hbm.1, bf16[32,24,512]{2,1,0:T(8,128)(2,1)} %bitcast.15, bf16[32,24,512]{2,1,0:T(8,128)(2,1)} %bitcast.16, ...), custom_call_target="tpu_custom_call" | custom-call | flops 11299999744 | bytes 14000000 | tf_op jit(solution)/shard_map/pallas_call | solution.py:483
  147.8 3.6 %shard_map.113 = (bf16[128,1792]{1,0:T(8,128)(2,1)}, f32[896,512]{1,0:T(8,128)}, f32[28,1,512]{2,1,0:T(1,128)}) custom-call(bf16[128,1792]{1,0:T(8,128)(2,1)} %get-tuple-element.9.grad_ref, f32[896,512]{1,0:T(8,128)} %get-tuple-element.10.sums_ref, f32[28,512]{1,0:T(8,128)} %get-tuple-element.11.scales_ref), custom_call_target="tpu_custom_call" | custom-call | tf_op jit(solution)/shard_map/pallas_call | solution.py:539

commit v4 on v3

--- a/solution.py
+++ b/solution.py
@@ -8,7 +8,7 @@
 MESH = pl.DeviceIdType.MESH
 BF16, F32 = jnp.bfloat16, jnp.float32
 
-EXPERTS, REPLICAS = 32, 4
+EXPERTS, REPLICAS, RING = 32, 4, 8
 TOKENS, TOP, CAP = 128, 4, 24
 D, GROUP, SHARD, BLOCK = 3584, 512, 896, 128
 HALF_D = D // 2
@@ -26,8 +26,9 @@
 def kernel(
     ids_ref, gates_ref, grad_hbm, gate_hbm, up_hbm, wg_hbm, wu_hbm, wd_hbm, res_hbm,
     grad_in_ref, sums_ref, scales_ref,
-    out, rcv, ret, part, part_got, wf, routed, pick, pick_t, grad, gate_pre, up_pre,
-    hid, fac_gate, fac_up, gate_grad, up_grad, res, corr, code_got, code_sum, maxima, total_in,
+    out, rcv, ret, part, part_got, wf, routed, pick, pick_t, info, grad, gate_pre, up_pre,
+    hid, fac_gate, fac_up, gate_grad, up_grad, res, corr, code_sum, maxima, total_in,
+    g_send, g_recv, i_send, i_recv,
     a_send, a_recv, f_send, f_recv, r_send, r_recv, w_send, w_recv, p_send, p_recv,
     m_send, m_recv, c_send, c_recv, l_sem,
 ):
@@ -42,8 +43,19 @@
     opposite = lax.rem(y + 2, REPLICAS)
     weights = (wd_hbm, wg_hbm, wu_hbm)
 
+    x, z = lax.div(me, RING), lax.rem(me, RING)
+
+    def turn(k):
+        return lax.div(k + 1, 2) * (1 - 2 * lax.rem(k, 2))
+
+    def place(x_, z_):
+        return lax.rem(x_ + 4, 4) * RING + lax.rem(z_ + RING, RING)
+
+    def source(s):
+        return place(x - lax.rem(s, 4), z + turn(lax.div(s, 4)))
+
     grad_copy = pltpu.make_async_copy(
-        grad_hbm.at[:, pl.ds(pl.multiple_of(core * HALF_D, HALF_D), HALF_D)], grad, l_sem.at[0]
+        grad_hbm.at[:, pl.ds(pl.multiple_of(core * HALF_D, HALF_D), HALF_D)], grad.at[0], l_sem.at[0]
     )
     res_copy = pltpu.make_async_copy(res_hbm, res, l_sem.at[3])
     own_weights = [pltpu.make_async_copy(weights[w], wf.at[w, y], l_sem.at[4 + w]) for w in range(3)]
@@ -79,34 +91,39 @@
         0.0,
     ).astype(BF16)
     earlier = dot(named.astype(BF16), before)
-    keys = []
     for k in range(TOP):
         id_k = ids[k : k + 1, :]
         slot_k = jnp.sum(jnp.where(id_k == expert_row, earlier, 0.0), axis=0, keepdims=True)
-        keys.append(id_k * 32.0 + slot_k)
-    row = lax.broadcasted_iota(jnp.int32, (ROWS_A, 1), 0)
-    in_row = jnp.bitwise_and(row, 15)
-    base = jnp.bitwise_and(me + jnp.right_shift(row, 4), EXPERTS - 1) * 32
-    key_a = (base + in_row).astype(F32)
-    key_b = (base + 16 + jnp.bitwise_and(row, 7)).astype(F32)
-    lower = in_row < 8
-    hot = jnp.zeros((ROWS_A, TOKENS), F32)
-    weigh = jnp.zeros((ROWS_A, TOKENS), F32)
-    hot_b = jnp.zeros((ROWS_A, TOKENS), F32)
-    weigh_b = jnp.zeros((ROWS_A, TOKENS), F32)
-    for k in range(TOP):
-        same = key_a == keys[k]
-        same_b = key_b == keys[k]
-        gate_k = gates_ref[k : k + 1, :]
-        hot = hot + jnp.where(same, 1.0, 0.0)
-        weigh = weigh + jnp.where(same, gate_k, 0.0)
-        hot_b = hot_b + jnp.where(same_b, 1.0, 0.0)
-        weigh_b = weigh_b + jnp.where(same_b, gate_k, 0.0)
-    gate_a = jnp.sum(weigh, axis=1, keepdims=True)
-    gate_b = jnp.sum(weigh_b, axis=1, keepdims=True)
-    pick[0] = hot.astype(BF16)
-    pick[1] = jnp.where(lower, hot_b, 0.0).astype(BF16)
-    pick[2] = jnp.where(lower, 0.0, hot_b).astype(BF16)
+        info[0, k : k + 1, :] = id_k * 32.0 + slot_k
+    info[0, TOP : 2 * TOP, :] = gates_ref[...]
+
+    def ring_copy(way, r):
+        chain = ((0, 1, 3, 5, 7), (0, 2, 4, 6, 7))[way]
+        hop, lo = r // 2, (r % 2 if way == 0 else 1 - r % 2) * 64
+        return pltpu.make_async_remote_copy(
+            src_ref=grad.at[chain[hop], pl.ds(lo, 64)],
+            dst_ref=grad.at[chain[hop + 1], pl.ds(lo, 64)],
+            send_sem=g_send.at[way * 7 + r],
+            recv_sem=g_recv.at[way * 7 + r],
+            device_id={"expert": place(x, z + 1 - 2 * way)},
+            device_id_type=MESH,
+        )
+
+    def ring_step(r):
+        for way in range(2):
+            ring_copy(way, r).wait_recv()
+            if r + 2 <= 6:
+                ring_copy(way, r + 2).start()
+
+    def info_copy(k):
+        return pltpu.make_async_remote_copy(
+            src_ref=info.at[0],
+            dst_ref=info.at[k],
+            send_sem=i_send.at[k],
+            recv_sem=i_recv.at[k],
+            device_id={"expert": place(x, z - turn(k))},
+            device_id_type=MESH,
+        )
 
     def weight_copy(number):
         if number < 12:
@@ -137,54 +154,76 @@
     pl.semaphore_wait(barrier, EXPERTS + 3)
     weights_start(0, 6, 1, 7, 2, 3, 4, 5)
 
+    for k in range(1, RING):
+        info_copy(k).start()
+    grad_copy.wait()
+    for r in range(2):
+        for way in range(2):
+            ring_copy(way, r).start()
+
     def dispatch(s):
         return pltpu.make_async_remote_copy(
             src_ref=out.at[s],
             dst_ref=rcv.at[core, s],
             send_sem=a_send.at[s],
             recv_sem=a_recv.at[s],
-            device_id={"expert": lax.rem(me + s, EXPERTS)},
-            device_id_type=MESH,
-        )
-
-    def start_dispatch(s, _):
-        dispatch(s).start()
-        return 0
-
-    grad_copy.wait()
-    own = pltpu.make_async_copy(out.at[0], rcv.at[core, 0], l_sem.at[7])
-    for q in range(4):
-        rows = pl.ds(q * 128, 128)
-        block = dot(pick[0, rows, :], grad[...]) * gate_a[q * 128 : (q + 1) * 128]
-        out[pl.ds(q * 8, 8), :, 0:HALF_D] = block.astype(BF16).reshape(8, 16, HALF_D)
-        block = dot(pick[1, rows, :], grad[:, 0:SHARD]) + dot(pick[2, rows, :], grad[:, SHARD:HALF_D])
-        block = block * gate_b[q * 128 : (q + 1) * 128]
-        out[pl.ds(q * 8, 8), :, HALF_D:WIDE] = block.astype(BF16).reshape(8, 16, SHARD)
-        lax.fori_loop(max(1, q * 8), q * 8 + 8, start_dispatch, 0)
-        if q == 0:
-            own.start()
-
-    def share(s):
-        return pltpu.make_async_remote_copy(
-            src_ref=rcv.at[core, s],
-            dst_ref=rcv.at[core, s],
-            send_sem=f_send.at[s],
-            recv_sem=f_recv.at[s],
+            device_id={"expert": place(x + lax.rem(s, 4), z)},
+            device_id_type=MESH,
+        )
+
+    def share(k):
+        block = rcv.at[core, pl.ds(4 * k, 4)]
+        return pltpu.make_async_remote_copy(
+            src_ref=block,
+            dst_ref=block,
+            send_sem=f_send.at[k],
+            recv_sem=f_recv.at[k],
             device_id={"tensor": other},
             device_id_type=MESH,
         )
 
-    def pass_on(s, _):
-        dispatch(s).wait_recv()
-        share(s).start()
-        return 0
-
-    def share_got(s, _):
-        share(s).wait()
-        return 0
-
-    own.wait()
-    share(0).start()
+    def pass_on(g):
+        for k in (2 * g, 2 * g + 1):
+            for j in range(1, 4):
+                dispatch(4 * k + j).wait_recv()
+            share(k).start()
+
+    def send_block(k):
+        if k > 0:
+            info_copy(k).wait_recv()
+        row = lax.broadcasted_iota(jnp.int32, (64, 1), 0)
+        in_row = jnp.bitwise_and(row, 15)
+        base = (jnp.bitwise_and(x + jnp.right_shift(row, 4), 3) * RING + z) * 32
+        key_a = (base + in_row).astype(F32)
+        key_b = (base + 16 + jnp.bitwise_and(row, 7)).astype(F32)
+        hot = weigh = hot_b = weigh_b = jnp.zeros((64, TOKENS), F32)
+        for p in range(TOP):
+            same = key_a == info[k, p : p + 1, :]
+            same_b = key_b == info[k, p : p + 1, :]
+            gate = info[k, TOP + p : TOP + p + 1, :]
+            hot = hot + jnp.where(same, 1.0, 0.0)
+            weigh = weigh + jnp.where(same, gate, 0.0)
+            hot_b = hot_b + jnp.where(same_b, 1.0, 0.0)
+            weigh_b = weigh_b + jnp.where(same_b, gate, 0.0)
+        gate_a = jnp.sum(weigh, axis=1, keepdims=True)
+        gate_b = jnp.sum(weigh_b, axis=1, keepdims=True)
+        low = jnp.concatenate([hot, jnp.where(in_row < 8, hot_b, 0.0)], axis=0).astype(BF16)
+        high = jnp.concatenate([hot, jnp.where(in_row < 8, 0.0, hot_b)], axis=0).astype(BF16)
+        left = dot(low, grad[k, :, 0:SHARD])
+        right = dot(high, grad[k, :, SHARD:HALF_D])
+        rows = (
+            (left[0:64] * gate_a, 0),
+            (right[0:64] * gate_a, SHARD),
+            ((left[64:128] + right[64:128]) * gate_b, HALF_D),
+        )
+        for value, at in rows:
+            value = value.astype(BF16).reshape(4, 16, SHARD)
+            rcv[core, 4 * k, :, at : at + SHARD] = value[0]
+            out[4 * k + 1 : 4 * k + 4, :, at : at + SHARD] = value[1:4]
+        for j in range(1, 4):
+            dispatch(4 * k + j).start()
+
+    send_block(0)
 
     for copy in saved:
         copy.wait()
@@ -192,9 +231,9 @@
     def activate(j, _):
         a, u = [], []
         for s in (2 * j, 2 * j + 1):
-            source = lax.rem(me + EXPERTS - s, EXPERTS)
-            a.append(gate_pre[source].astype(F32))
-            u.append(up_pre[source].astype(F32))
+            block = source(s)
+            a.append(gate_pre[block].astype(F32))
+            u.append(up_pre[block].astype(F32))
         first = lax.div(j, 4) * TILE
         step = lax.rem(j, 4)
         for lo, hi, at in ((0, 16, first + step * 32), (16, 24, first + 128 + step * 16)):
@@ -214,7 +253,8 @@
         return pl.ds(pl.multiple_of(g * TILE, TILE), TILE)
 
     def unfold(g):
-        lax.fori_loop(g * 8, g * 8 + 8, share_got, 0)
+        for k in (2 * g, 2 * g + 1):
+            share(k).wait()
         for h in range(2):
             routed[h, g * TILE : g * TILE + 128, :] = rcv[h, g * 8 : g * 8 + 8, :, 0:HALF_D].reshape(128, HALF_D)
             raw = rcv[h, g * 8 : g * 8 + 8, :, HALF_D:WIDE].astype(F32).reshape(8, 2, 8, SHARD)
@@ -229,12 +269,16 @@
     def hidden_grads(g, _):
         rows = tile_of(g)
         total = dot(routed[0, rows, :], w_half(0, 0)) + dot(routed[1, rows, :], w_half(0, 1))
-        gate_grad[rows, :] = (total * fac_gate[rows, :]).astype(BF16)
-        up_grad[rows, :] = (total * fac_up[rows, :]).astype(BF16)
+        by_gate = (total * fac_gate[rows, :]).astype(BF16)
+        by_up = (total * fac_up[rows, :]).astype(BF16)
+        for lo, hi, to in ((0, 128, g * 128), (128, TILE, ROWS_A + g * 64)):
+            to = pl.ds(pl.multiple_of(to, 64), hi - lo)
+            gate_grad[to, :] = by_gate[lo:hi]
+            up_grad[to, :] = by_up[lo:hi]
         return 0
 
-    def correct(lo, hi, first, last):
-        for h in range(2):
+    def correct(lo, hi, first, last, halves):
+        for h in halves:
             def step(t, _, h=h):
                 columns = pl.ds(pl.multiple_of(t * 256, 256), 256)
                 rows = pl.ds(pl.multiple_of(h * HALF_D + t * 256, 256), 256)
@@ -249,112 +293,126 @@
 
             lax.fori_loop(0, 7, step, 0)
 
-    def swap(stage, g):
-        block = pl.ds(g * 8, 8)
-        return pltpu.make_async_remote_copy(
-            src_ref=part.at[stage, block],
+    SPANS = ((0, SHARD), (SHARD, WIDE))
+
+    def half_of(stage):
+        return near if stage == 0 else 1 - near
+
+    def swap(stage, phase, g):
+        lo, hi = SPANS[phase]
+        block = (pl.ds(g * 8, 8), slice(None), slice(lo, hi))
+        return pltpu.make_async_remote_copy(
+            src_ref=part.at[(stage,) + block],
             dst_ref=part_got.at[block],
-            send_sem=p_send.at[g],
-            recv_sem=p_recv.at[g],
+            send_sem=p_send.at[phase * 4 + g],
+            recv_sem=p_recv.at[phase * 4 + g],
             device_id={"tensor": other},
             device_id_type=MESH,
         )
 
-    def partial(stage):
-        half = near if stage == 0 else 1 - near
-
-        def group(g, _):
-            rows = tile_of(g)
-            values = []
-            for q in range(2):
-                s = 2 * half + q
-                value = dot(gate_grad[rows, :], wf[1, s], ((1,), (1,))) + dot(
-                    up_grad[rows, :], wf[2, s], ((1,), (1,))
+    def partial(stage, phase):
+        shards = ((y, pair), (next_, opposite))[stage]
+
+        for lo in range(0, SHARD, 256):
+            hi = min(lo + 256, SHARD)
+
+            def value(rows, s, lo=lo, hi=hi):
+                return dot(gate_grad[rows, :], wf[1, s, lo:hi, :], ((1,), (1,))) + dot(
+                    up_grad[rows, :], wf[2, s, lo:hi, :], ((1,), (1,))
                 )
-                part[stage, pl.ds(g * 8, 8), :, q * SHARD : (q + 1) * SHARD] = (
-                    value[0:128].astype(BF16).reshape(8, 16, SHARD)
-                )
-                values.append(value[128:TILE].reshape(8, 1, 8, SHARD))
-            both = jnp.concatenate(values, axis=1).reshape(8, 16, SHARD)
-            part[stage, pl.ds(g * 8, 8), :, HALF_D:WIDE] = both.astype(BF16)
-
-            @pl.when(half != core)
-            def _():
-                swap(stage, g).start()
-
+
+            at = phase * SHARD + lo
+            part[stage, :, :, at : at + hi - lo] = (
+                value(slice(0, ROWS_A), shards[phase]).astype(BF16).reshape(EXPERTS, 16, hi - lo)
+            )
+            if phase == 1:
+                both = [value(slice(ROWS_A, SLOTS), s).reshape(EXPERTS, 1, 8, hi - lo) for s in shards]
+                both = jnp.concatenate(both, axis=1).reshape(EXPERTS, 16, hi - lo)
+                part[stage, :, :, HALF_D + lo : HALF_D + hi] = both.astype(BF16)
+
+        @pl.when(half_of(stage) != core)
+        def _():
+            for g in range(4):
+                swap(stage, phase, g).start()
+
+    def give_back(phase, s):
+        lo, hi = SPANS[phase]
+        return pltpu.make_async_remote_copy(
+            src_ref=out.at[s, :, lo:hi],
+            dst_ref=ret.at[s, :, lo:hi],
+            send_sem=r_send.at[phase * EXPERTS + s],
+            recv_sem=r_recv.at[phase * EXPERTS + s],
+            device_id={"expert": source(s)},
+            device_id_type=MESH,
+        )
+
+    def send_back(stage, phase):
+        lo, hi = SPANS[phase]
+
+        def summed(s):
+            return (part[stage, s, :, lo:hi].astype(F32) + part_got[s, :, lo:hi].astype(F32)).astype(BF16)
+
+        def one(s, _):
+            out[s, :, lo:hi] = summed(s)
+            give_back(phase, s).start()
             return 0
 
-        return group
-
-    def give_back(s):
-        return pltpu.make_async_remote_copy(
-            src_ref=out.at[s],
-            dst_ref=ret.at[s],
-            send_sem=r_send.at[s],
-            recv_sem=r_recv.at[s],
-            device_id={"expert": lax.rem(me + EXPERTS - s, EXPERTS)},
-            device_id_type=MESH,
-        )
-
-    def send_back(stage, lo, hi):
-        half = near if stage == 0 else 1 - near
-
-        def summed(s):
-            return (part[stage, s].astype(F32) + part_got[s].astype(F32)).astype(BF16)
-
-        def one(s, _):
-            dispatch(s).wait_send()
-            out[s] = summed(s)
-            give_back(s).start()
-            return 0
-
-        @pl.when(half == core)
+        @pl.when(half_of(stage) == core)
         def _():
-            for g in range(lo, hi):
-                swap(stage, g).wait_recv()
+            for g in range(4):
+                swap(stage, phase, g).wait_recv()
                 if g == 0:
-                    ret[0] = summed(0)
+                    ret[0, :, lo:hi] = summed(0)
                 lax.fori_loop(max(1, g * 8), g * 8 + 8, one, 0)
 
-    lax.fori_loop(1, 3, pass_on, 0)
+    ring_step(0)
+    ring_step(1)
     weights_wait(0)
     weights_start(12)
-    lax.fori_loop(3, 6, pass_on, 0)
+    send_block(1)
+    send_block(2)
+    ring_step(2)
+    ring_step(3)
     weights_wait(1)
-    weights_start(13, 8, 9, 11, 10)
-    for j in range(3):
-        pick_t[j] = jnp.transpose(pick[j].astype(F32)).astype(BF16)
-    lax.fori_loop(6, 8, pass_on, 0)
+    weights_start(13, 8, 9)
+    send_block(3)
+    send_block(4)
+    pass_on(0)
+    ring_step(4)
     unfold(0)
-    lax.fori_loop(8, 16, pass_on, 0)
+    ring_step(5)
+    send_block(5)
+    send_block(6)
+    pass_on(1)
     unfold(1)
+    res_copy.wait()
+    correct(0, 2 * TILE, True, False, (0,))
+    ring_step(6)
+    send_block(7)
+    pass_on(2)
+    unfold(2)
+    pass_on(3)
+    correct(0, 2 * TILE, True, False, (1,))
+    unfold(3)
     own_weights[0].wait()
     weights_wait(6, 7, 12, 13)
-    lax.fori_loop(0, 2, hidden_grads, 0)
-    res_copy.wait()
-    correct(0, 2 * TILE, True, False)
-    lax.fori_loop(16, 24, pass_on, 0)
-    unfold(2)
-    hidden_grads(2, 0)
-    weights_wait(8, 4)
-    weights_start(15, 14)
-    lax.fori_loop(24, 28, pass_on, 0)
+    lax.fori_loop(0, 4, hidden_grads, 0)
     own_weights[1].wait()
     own_weights[2].wait()
-    weights_wait(2, 3, 5)
-    lax.fori_loop(0, 2, partial(0), 0)
-    lax.fori_loop(28, EXPERTS, pass_on, 0)
-    partial(0)(2, 0)
-    weights_wait(9)
-    weights_start(16)
-    send_back(0, 0, 3)
-    unfold(3)
-    hidden_grads(3, 0)
-    partial(0)(3, 0)
-    send_back(0, 3, 4)
-    weights_wait(11)
-    weights_start(17)
-    correct(2 * TILE, SLOTS, False, True)
+    partial(0, 0)
+    weights_start(11)
+
+    def dispatched(i, _):
+        dispatch(lax.div(i, 3) * 4 + 1 + lax.rem(i, 3)).wait_send()
+        return 0
+
+    lax.fori_loop(0, 24, dispatched, 0)
+    send_back(0, 0)
+    weights_wait(8, 4)
+    weights_start(15)
+    correct(2 * TILE, SLOTS, False, True, (0, 1))
+    for number in (12, 13):
+        weight_copy(number).wait_send()
 
     def max_copy(i):
         return pltpu.make_async_remote_copy(
@@ -368,6 +426,32 @@
 
     for i in range(3):
         max_copy(i).start()
+    weights_start(10, 14)
+    weights_wait(2, 3, 5)
+    weights_wait(9)
+    weights_start(16)
+    partial(0, 1)
+    send_back(0, 1)
+
+    row = lax.broadcasted_iota(jnp.int32, (ROWS_A, 1), 0)
+    in_row = jnp.bitwise_and(row, 15)
+    ring = jnp.right_shift(row, 6)
+    turned = jnp.right_shift(ring + 1, 1) * (1 - 2 * jnp.bitwise_and(ring, 1))
+    expert = jnp.bitwise_and(x + jnp.right_shift(row, 4), 3) * RING + jnp.bitwise_and(z - turned, RING - 1)
+    key_a = (expert * 32 + in_row).astype(F32)
+    key_b = (expert * 32 + 16 + jnp.bitwise_and(row, 7)).astype(F32)
+    hot = hot_b = jnp.zeros((ROWS_A, TOKENS), F32)
+    for p in range(TOP):
+        hot = hot + jnp.where(key_a == info[0, p : p + 1, :], 1.0, 0.0)
+        hot_b = hot_b + jnp.where(key_b == info[0, p : p + 1, :], 1.0, 0.0)
+    pick[0] = hot
+    pick[1] = jnp.where(in_row < 8, hot_b, 0.0)
+    pick[2] = jnp.where(in_row < 8, 0.0, hot_b)
+    for j in range(3):
+        pick_t[j] = jnp.transpose(pick[j]).astype(BF16)
+
+    weights_wait(11)
+    weights_start(17)
     for i in range(3):
         max_copy(i).wait()
     largest = jnp.maximum(jnp.maximum(maxima[0], maxima[1]), jnp.maximum(maxima[2], maxima[3]))
@@ -382,6 +466,9 @@
 
     def code_rows(owner, lo):
         return pl.ds(pl.multiple_of(owner * SHARD + lo, CUT), CUT)
+
+    def code_got(i):
+        return wf.at[0, i // 2, pl.ds(i % 2 * CUT, CUT)]
 
     def code_copy(i):
         peer = (pair, next_, pair, next_, pair, next_)[i]
@@ -390,7 +477,7 @@
         src = res.at[code_rows(owner, lo)] if i < 4 else code_sum.at[i - 4]
         return pltpu.make_async_remote_copy(
             src_ref=src,
-            dst_ref=code_got.at[i],
+            dst_ref=code_got(i),
             send_sem=c_send.at[i],
             recv_sem=c_recv.at[i],
             device_id={"replica": peer},
@@ -403,17 +490,21 @@
     def code_pass(i):
         code_copy(1 - i).wait_recv()
         owner, lo = ((pair, 0), (next_, CUT))[i]
-        code_sum[i] = (res[code_rows(owner, lo), :].astype(F32) + code_got[1 - i].astype(F32)).astype(BF16)
+        code_sum[i] = (res[code_rows(owner, lo), :].astype(F32) + code_got(1 - i)[...].astype(F32)).astype(BF16)
         code_copy(4 + i).start()
 
-    weights_wait(10, 14, 15, 16, 17)
-    lax.fori_loop(0, 4, partial(1), 0)
-    send_back(1, 0, 4)
+    weights_wait(10)
+    partial(1, 0)
+    send_back(1, 0)
+    weights_wait(14, 15, 16, 17)
+    partial(1, 1)
+    send_back(1, 1)
     for i in range(2):
         code_pass(i)
 
     def came_back(s, _):
-        give_back(s).wait()
+        give_back(0, s).wait()
+        give_back(1, s).wait()
         return 0
 
     def combine(g):
@@ -428,7 +519,9 @@
             if g < 3:
                 total_in[:, columns] = total
             else:
-                grad_in_ref[:, columns] = total.astype(BF16)
+                shard = jnp.where(core == near, (y, pair)[q], (next_, opposite)[q])
+                to = pl.ds(pl.multiple_of(lax.rem(shard, 2) * SHARD, SHARD), SHARD)
+                grad_in_ref[:, to] = total.astype(BF16)
 
     for g in range(3):
         lax.fori_loop(max(1, g * 8), g * 8 + 8, came_back, 0)
@@ -442,7 +535,7 @@
         for lo, first, second in ((0, 3, 4), (CUT, 2, 5)):
             total = res[pl.ds(pl.multiple_of(y * SHARD + lo + t * 64, 64), 64), :].astype(F32)
             for i in (first, second):
-                total = total + code_got[i, rows, :].astype(F32)
+                total = total + wf[0, i // 2, pl.ds(pl.multiple_of(i % 2 * CUT + t * 64, 64), 64), :].astype(F32)
             sums_ref[pl.ds(pl.multiple_of(lo + t * 64, 64), 64), :] = total
         return 0
 
@@ -451,14 +544,21 @@
     combine(3)
 
     for number in range(18):
-        weight_copy(number).wait_send()
+        if number not in (12, 13):
+            weight_copy(number).wait_send()
+    for k in range(1, RING):
+        info_copy(k).wait_send()
+    for r in range(7):
+        for way in range(2):
+            ring_copy(way, r).wait_send()
     for i in range(6):
         code_copy(i).wait_send()
     for stage, half in ((0, near), (1, 1 - near)):
         @pl.when(half != core)
         def _(stage=stage):
             for g in range(4):
-                swap(stage, g).wait_send()
+                for phase in range(2):
+                    swap(stage, phase, g).wait_send()
 
 
 def hand_out(grad_ref, sums_ref, scales_ref, grad_out, sums_out, scales_out, sem):
@@ -497,9 +597,10 @@
             pltpu.VMEM(message, BF16),
             pltpu.VMEM((3, REPLICAS, SHARD, GROUP), BF16),
             pltpu.VMEM((2, SLOTS, HALF_D), BF16),
-            pltpu.VMEM((3, ROWS_A, TOKENS), BF16),
+            pltpu.VMEM((3, ROWS_A, TOKENS), F32),
             pltpu.VMEM((3, TOKENS, ROWS_A), BF16),
-            pltpu.VMEM((TOKENS, HALF_D), BF16),
+            pltpu.VMEM((RING, 2 * TOP, TOKENS), F32),
+            pltpu.VMEM((RING, TOKENS, HALF_D), BF16),
             pltpu.VMEM((EXPERTS, CAP, GROUP), BF16),
             pltpu.VMEM((EXPERTS, CAP, GROUP), BF16),
             pltpu.VMEM((SLOTS, GROUP), BF16),
@@ -509,20 +610,23 @@
             pltpu.VMEM((SLOTS, GROUP), BF16),
             pltpu.VMEM((D, GROUP), BF16),
             pltpu.VMEM((D, GROUP), F32),
-            pltpu.VMEM((6, CUT, GROUP), BF16),
             pltpu.VMEM((2, CUT, GROUP), BF16),
             pltpu.VMEM((REPLICAS, D // BLOCK, GROUP), F32),
             pltpu.VMEM((TOKENS, HALF_D), F32),
+            dma((14,)),
+            dma((14,)),
+            dma((RING,)),
+            dma((RING,)),
             dma((EXPERTS,)),
             dma((EXPERTS,)),
             dma((EXPERTS,)),
             dma((EXPERTS,)),
-            dma((EXPERTS,)),
-            dma((EXPERTS,)),
+            dma((2 * EXPERTS,)),
+            dma((2 * EXPERTS,)),
             dma((18,)),
             dma((18,)),
-            dma((4,)),
-            dma((4,)),
+            dma((8,)),
+            dma((8,)),
             dma((3,)),
             dma((3,)),
             dma((6,)),

time: 152 us -> 145 us (0.954)
  Pallas kernels: 151 us -> 145 us
    pallas_call x1, Pallas kernels: 147 us -> 141 us  [local(): pl.pallas_call(kernel, out_shape=(jax.ShapeDtypeStruct((TOKENS, HALF_D),...]
where the time goes in v4:
time: 145 us
  Pallas kernels  145 us (100%)
    pallas_call x1, Pallas kernels, local(): pl.pallas_call(kernel, out_shape=(jax.ShapeDtypeStruct((TOKENS, HALF_D),...  141 us
    pallas_call x1, Pallas kernels, local(): pl.pallas_call(hand_out, out_shape=(jax.ShapeDtypeStruct((TOKENS, HALF_D)...  3.59 us

profile of v4, /device:TPU:1, one launch (start us, length us, event | category | flops | bytes accessed | tf_op | source)
XLA Modules:
  0.0 145.4 jit_solution(1054999791560272150)
XLA Ops:
  0.6 141.1 %shard_map.112 = (bf16[128,1792]{1,0:T(8,128)(2,1)}, f32[896,512]{1,0:T(8,128)}, f32[28,512]{1,0:T(8,128)}) custom-call(s32[4,128]{1,0:T(4,128)} %bitcast.18, f32[4,128]{1,0:T(4,128)} %bitcast.19, bf16[128,3584]{1,0:T(8,128)(2,1)} %grad_hbm.1, bf16[32,24,512]{2,1,0:T(8,128)(2,1)} %bitcast.15, bf16[32,24,512]{2,1,0:T(8,128)(2,1)} %bitcast.16, ...), custom_call_target="tpu_custom_call" | custom-call | flops 11299999744 | bytes 14000000 | tf_op jit(solution)/shard_map/pallas_call | solution.py:583
  141.8 3.6 %shard_map.113 = (bf16[128,1792]{1,0:T(8,128)(2,1)}, f32[896,512]{1,0:T(8,128)}, f32[28,1,512]{2,1,0:T(1,128)}) custom-call(bf16[128,1792]{1,0:T(8,128)(2,1)} %get-tuple-element.9.grad_ref, f32[896,512]{1,0:T(8,128)} %get-tuple-element.10.sums_ref, f32[28,512]{1,0:T(8,128)} %get-tuple-element.11.scales_ref), custom_call_target="tpu_custom_call" | custom-call | tf_op jit(solution)/shard_map/pallas_call | solution.py:643

commit v5 on v4

--- a/solution.py
+++ b/solution.py
@@ -25,9 +25,9 @@
 
 def kernel(
     ids_ref, gates_ref, grad_hbm, gate_hbm, up_hbm, wg_hbm, wu_hbm, wd_hbm, res_hbm,
-    grad_in_ref, sums_ref, scales_ref,
-    out, rcv, ret, part, part_got, wf, routed, pick, pick_t, info, grad, gate_pre, up_pre,
-    hid, fac_gate, fac_up, gate_grad, up_grad, res, corr, code_sum, maxima, total_in,
+    grad_in_hbm, sums_hbm, scales_hbm,
+    grad_in_ref, sums_ref, scales_ref, out, rcv, ret, part, part_got, wf, routed, pick, pick_t, info, grad, gate_pre, up_pre,
+    hid, fac_gate, fac_up, gate_grad, up_grad, res, corr, code_sum, own_max, maxima, total_in,
     g_send, g_recv, i_send, i_recv,
     a_send, a_recv, f_send, f_recv, r_send, r_recv, w_send, w_recv, p_send, p_recv,
     m_send, m_recv, c_send, c_recv, l_sem,
@@ -63,9 +63,6 @@
         pltpu.make_async_copy(gate_hbm, gate_pre, l_sem.at[1]),
         pltpu.make_async_copy(up_hbm, up_pre, l_sem.at[2]),
     ]
-    for copy in [grad_copy] + saved + own_weights + [res_copy]:
-        copy.start()
-
     barrier = pltpu.get_barrier_semaphore()
 
     def greet(i, _):
@@ -78,6 +75,38 @@
         pl.semaphore_signal(barrier, inc=1, device_id={"replica": peer}, device_id_type=MESH)
     pl.semaphore_signal(barrier, inc=1, device_id={"tensor": other}, device_id_type=MESH)
     lax.fori_loop(1, EXPERTS, greet, 0)
+    for copy in [grad_copy] + saved + own_weights + [res_copy]:
+        copy.start()
+
+    def weight_copy(number):
+        if number < 12:
+            w, lo = number % 6 // 2, number % 2 * CUT
+            owner, peer = y, (pair if number < 6 else next_)
+            src = weights[w].at[pl.ds(lo, CUT)]
+        else:
+            w, lo = ((0, 0), (0, CUT), (2, 0), (1, 0), (1, CUT), (2, CUT))[number - 12]
+            owner, peer = (pair, next_) if number < 15 else (next_, pair)
+            src = wf.at[w, owner, pl.ds(lo, CUT)]
+        return pltpu.make_async_remote_copy(
+            src_ref=src,
+            dst_ref=wf.at[w, owner, pl.ds(lo, CUT)],
+            send_sem=w_send.at[number],
+            recv_sem=w_recv.at[number],
+            device_id={"replica": peer},
+            device_id_type=MESH,
+        )
+
+    def weights_start(*numbers):
+        for number in numbers:
+            weight_copy(number).start()
+
+    def weights_wait(*numbers):
+        for number in numbers:
+            weight_copy(number).wait_recv()
+
+
+    pl.semaphore_wait(barrier, EXPERTS + 3)
+    weights_start(0, 6, 1, 7, 2, 3, 4, 5)
 
     ids = ids_ref[...].astype(F32)
     expert_row = lax.broadcasted_iota(jnp.int32, (EXPERTS, TOKENS), 0).astype(F32)
@@ -124,35 +153,6 @@
             device_id={"expert": place(x, z - turn(k))},
             device_id_type=MESH,
         )
-
-    def weight_copy(number):
-        if number < 12:
-            w, lo = number % 6 // 2, number % 2 * CUT
-            owner, peer = y, (pair if number < 6 else next_)
-            src = weights[w].at[pl.ds(lo, CUT)]
-        else:
-            w, lo = ((0, 0), (0, CUT), (2, 0), (1, 0), (1, CUT), (2, CUT))[number - 12]
-            owner, peer = (pair, next_) if number < 15 else (next_, pair)
-            src = wf.at[w, owner, pl.ds(lo, CUT)]
-        return pltpu.make_async_remote_copy(
-            src_ref=src,
-            dst_ref=wf.at[w, owner, pl.ds(lo, CUT)],
-            send_sem=w_send.at[number],
-            recv_sem=w_recv.at[number],
-            device_id={"replica": peer},
-            device_id_type=MESH,
-        )
-
-    def weights_start(*numbers):
-        for number in numbers:
-            weight_copy(number).start()
-
-    def weights_wait(*numbers):
-        for number in numbers:
-            weight_copy(number).wait_recv()
-
-    pl.semaphore_wait(barrier, EXPERTS + 3)
-    weights_start(0, 6, 1, 7, 2, 3, 4, 5)
 
     for k in range(1, RING):
         info_copy(k).start()
@@ -288,7 +288,7 @@
                 if last:
                     for b in range(2):
                         top = jnp.max(jnp.abs(total[b * BLOCK : (b + 1) * BLOCK]), axis=0, keepdims=True)
-                        maxima[y, pl.ds(h * 14 + t * 2 + b, 1), :] = top
+                        own_max[pl.ds(h * 14 + t * 2 + b, 1), :] = top
                 return 0
 
             lax.fori_loop(0, 7, step, 0)
@@ -414,6 +414,9 @@
     for number in (12, 13):
         weight_copy(number).wait_send()
 
+    own_max[D // BLOCK :, :] = jnp.zeros((32 - D // BLOCK, GROUP), F32)
+    maxima[y] = own_max[...].astype(BF16)
+
     def max_copy(i):
         return pltpu.make_async_remote_copy(
             src_ref=maxima.at[y],
@@ -454,8 +457,12 @@
     weights_start(17)
     for i in range(3):
         max_copy(i).wait()
-    largest = jnp.maximum(jnp.maximum(maxima[0], maxima[1]), jnp.maximum(maxima[2], maxima[3]))
-    scales_ref[...] = largest + 1e-6
+    largest = maxima[0].astype(F32)
+    for r in range(1, REPLICAS):
+        largest = jnp.maximum(largest, maxima[r].astype(F32))
+    scales_ref[...] = largest[0 : D // BLOCK] + 1e-6
+    results = [pltpu.make_async_copy(scales_ref, scales_hbm, l_sem.at[7])]
+    results[0].start()
 
     def code(b, _):
         rows = pl.ds(pl.multiple_of(b * BLOCK, BLOCK), BLOCK)
@@ -527,21 +534,28 @@
         lax.fori_loop(max(1, g * 8), g * 8 + 8, came_back, 0)
         combine(g)
 
-    for i in range(2, 6):
-        code_copy(i).wait_recv()
-
-    def add_codes(t, _):
-        rows = pl.ds(pl.multiple_of(t * 64, 64), 64)
-        for lo, first, second in ((0, 3, 4), (CUT, 2, 5)):
+    lax.fori_loop(24, EXPERTS, came_back, 0)
+    combine(3)
+    results.append(pltpu.make_async_copy(grad_in_ref, grad_in_hbm, l_sem.at[8]))
+    results[1].start()
+
+    for lo, first, second in ((0, 3, 4), (CUT, 2, 5)):
+        code_copy(first).wait_recv()
+        code_copy(second).wait_recv()
+
+        def add_codes(t, _, lo=lo, first=first, second=second):
+            rows = pl.ds(pl.multiple_of(lo + t * 64, 64), 64)
             total = res[pl.ds(pl.multiple_of(y * SHARD + lo + t * 64, 64), 64), :].astype(F32)
             for i in (first, second):
-                total = total + wf[0, i // 2, pl.ds(pl.multiple_of(i % 2 * CUT + t * 64, 64), 64), :].astype(F32)
-            sums_ref[pl.ds(pl.multiple_of(lo + t * 64, 64), 64), :] = total
-        return 0
-
-    lax.fori_loop(0, CUT // 64, add_codes, 0)
-    lax.fori_loop(24, EXPERTS, came_back, 0)
-    combine(3)
+                got = pl.ds(pl.multiple_of(i % 2 * CUT + t * 64, 64), 64)
+                total = total + wf[0, i // 2, got, :].astype(F32)
+            sums_ref[rows, :] = total
+            return 0
+
+        lax.fori_loop(0, CUT // 64, add_codes, 0)
+        rows = pl.ds(lo, CUT)
+        results.append(pltpu.make_async_copy(sums_ref.at[rows], sums_hbm.at[rows], l_sem.at[9 + lo // CUT]))
+        results[-1].start()
 
     for number in range(18):
         if number not in (12, 13):
@@ -559,18 +573,28 @@
             for g in range(4):
                 for phase in range(2):
                     swap(stage, phase, g).wait_send()
-
-
-def hand_out(grad_ref, sums_ref, scales_ref, grad_out, sums_out, scales_out, sem):
-    copies = [
-        pltpu.make_async_copy(grad_ref, grad_out, sem.at[0]),
-        pltpu.make_async_copy(sums_ref, sums_out, sem.at[1]),
-    ]
-    for copy in copies:
+    for copy in results:
+        copy.wait()
+
+
+def hand_out(grad_ref, sums_ref, scales_ref, grad_out, sums_out, scales_out, grad, sums, scales, flat, come, go):
+    half = SHARD // 2
+    pieces = [(scales_ref, scales, flat, scales_out), (grad_ref, grad, grad, grad_out)]
+    for t in range(2):
+        rows = pl.ds(t * half, half)
+        pieces.append((sums_ref.at[rows], sums.at[rows], sums.at[rows], sums_out.at[rows]))
+    into = [pltpu.make_async_copy(p[0], p[1], come.at[i]) for i, p in enumerate(pieces)]
+    away = [pltpu.make_async_copy(p[2], p[3], go.at[i]) for i, p in enumerate(pieces)]
+    for copy in into:
         copy.start()
+    into[0].wait()
     for b in range(D // BLOCK):
-        scales_out[b] = scales_ref[b : b + 1, :]
-    for copy in copies:
+        flat[b] = scales[b : b + 1, :]
+    away[0].start()
+    for first, second in zip(into[1:], away[1:]):
+        first.wait()
+        second.start()
+    for copy in away:
         copy.wait()
 
 
@@ -588,8 +612,11 @@
             jax.ShapeDtypeStruct((D // BLOCK, GROUP), F32),
         ),
         in_specs=[whole, whole] + [hbm] * 7,
-        out_specs=(whole, whole, whole),
+        out_specs=(hbm, hbm, hbm),
         scratch_shapes=[
+            pltpu.VMEM((TOKENS, HALF_D), BF16),
+            pltpu.VMEM((SHARD, GROUP), F32),
+            pltpu.VMEM((D // BLOCK, GROUP), F32),
             pltpu.VMEM(message, BF16),
             pltpu.VMEM((2,) + message, BF16),
             pltpu.VMEM(message, BF16),
@@ -611,7 +638,8 @@
             pltpu.VMEM((D, GROUP), BF16),
             pltpu.VMEM((D, GROUP), F32),
             pltpu.VMEM((2, CUT, GROUP), BF16),
-            pltpu.VMEM((REPLICAS, D // BLOCK, GROUP), F32),
+            pltpu.VMEM((32, GROUP), F32),
+            pltpu.VMEM((REPLICAS, 32, GROUP), BF16),
             pltpu.VMEM((TOKENS, HALF_D), F32),
             dma((14,)),
             dma((14,)),
@@ -631,7 +659,7 @@
             dma((3,)),
             dma((6,)),
             dma((6,)),
-            dma((8,)),
+            dma((11,)),
         ],
         compiler_params=pltpu.CompilerParams(
             collective_id=0, has_side_effects=True, vmem_limit_bytes=62 * 2**20
@@ -647,9 +675,17 @@
             jax.ShapeDtypeStruct((SHARD, GROUP), F32),
             jax.ShapeDtypeStruct((D // BLOCK, 1, GROUP), F32),
         ),
-        in_specs=[whole] * 3,
-        out_specs=(hbm, hbm, whole),
-        scratch_shapes=[dma((2,))],
+        in_specs=[hbm, hbm, hbm],
+        out_specs=(hbm, hbm, hbm),
+        scratch_shapes=[
+            pltpu.VMEM((TOKENS, HALF_D), BF16),
+            pltpu.VMEM((SHARD, GROUP), F32),
+            pltpu.VMEM((D // BLOCK, GROUP), F32),
+            pltpu.VMEM((D // BLOCK, 1, GROUP), F32),
+            dma((4,)),
+            dma((4,)),
+        ],
+        compiler_params=pltpu.CompilerParams(vmem_limit_bytes=60 * 2**20),
     )(grad_in, code_sums, scales)
     return grad_in, code_sums[None], scales.reshape(1, D // BLOCK, GROUP)
 

time: 145 us -> 142 us (0.979)
  Pallas kernels: 145 us -> 141 us
    pallas_call x1, Pallas kernels: 141 us -> 138 us  [local(): pl.pallas_call(kernel, out_shape=(jax.ShapeDtypeStruct((TOKENS, HALF_D),...]
where the time goes in v5:
time: 142 us; the launch traced here: 141 us
  Pallas kernels  141 us (99%)
    pallas_call x1, Pallas kernels, local(): pl.pallas_call(kernel, out_shape=(jax.ShapeDtypeStruct((TOKENS, HALF_D),...  138 us

profile of v5, /device:TPU:1, one launch (start us, length us, event | category | flops | bytes accessed | tf_op | source)
XLA Modules:
  0.0 141.3 jit_solution(13510539786031113137)
XLA Ops:
  0.6 138.0 %shard_map.112 = (bf16[128,1792]{1,0:T(8,128)(2,1)}, f32[896,512]{1,0:T(8,128)}, f32[28,512]{1,0:T(8,128)}) custom-call(s32[4,128]{1,0:T(4,128)} %bitcast.18, f32[4,128]{1,0:T(4,128)} %bitcast.19, bf16[128,3584]{1,0:T(8,128)(2,1)} %grad_hbm.1, bf16[32,24,512]{2,1,0:T(8,128)(2,1)} %bitcast.15, bf16[32,24,512]{2,1,0:T(8,128)(2,1)} %bitcast.16, ...), custom_call_target="tpu_custom_call" | custom-call | flops 11299999744 | bytes 14000000 | tf_op jit(solution)/shard_map/pallas_call | solution.py:607
  138.7 2.6 %shard_map.113 = (bf16[128,1792]{1,0:T(8,128)(2,1)}, f32[896,512]{1,0:T(8,128)}, f32[28,1,512]{2,1,0:T(1,128)}) custom-call(bf16[128,1792]{1,0:T(8,128)(2,1)} %get-tuple-element.9.grad_ref, f32[896,512]{1,0:T(8,128)} %get-tuple-element.10.sums_ref, f32[28,512]{1,0:T(8,128)} %get-tuple-element.11.scales_ref), custom_call_target="tpu_custom_call" | custom-call | tf_op jit(solution)/shard_map/pallas_call | solution.py:671

commit v6 on v5

--- a/solution.py
+++ b/solution.py
@@ -75,9 +75,7 @@
         pl.semaphore_signal(barrier, inc=1, device_id={"replica": peer}, device_id_type=MESH)
     pl.semaphore_signal(barrier, inc=1, device_id={"tensor": other}, device_id_type=MESH)
     lax.fori_loop(1, EXPERTS, greet, 0)
-    for copy in [grad_copy] + saved + own_weights + [res_copy]:
-        copy.start()
-
+    grad_copy.start()
     def weight_copy(number):
         if number < 12:
             w, lo = number % 6 // 2, number % 2 * CUT
@@ -107,6 +105,8 @@
 
     pl.semaphore_wait(barrier, EXPERTS + 3)
     weights_start(0, 6, 1, 7, 2, 3, 4, 5)
+    for copy in saved + own_weights + [res_copy]:
+        copy.start()
 
     ids = ids_ref[...].astype(F32)
     expert_row = lax.broadcasted_iota(jnp.int32, (EXPERTS, TOKENS), 0).astype(F32)
@@ -471,23 +471,28 @@
 
     lax.fori_loop(0, D // BLOCK, code, 0)
 
-    def code_rows(owner, lo):
-        return pl.ds(pl.multiple_of(owner * SHARD + lo, CUT), CUT)
+    PART = CUT // 2
+
+    def code_rows(owner, lo, n):
+        return pl.ds(pl.multiple_of(owner * SHARD + lo, PART), n)
 
     def code_got(i):
-        return wf.at[0, i // 2, pl.ds(i % 2 * CUT, CUT)]
+        if i < 4:
+            return wf.at[0, i // 2, pl.ds(i % 2 * CUT, CUT)]
+        return wf.at[0, 2, pl.ds(i % 2 * CUT + i // 6 * PART, PART)]
 
     def code_copy(i):
-        peer = (pair, next_, pair, next_, pair, next_)[i]
-        owner = (opposite, opposite, pair, next_, pair, next_)[i]
-        lo = (CUT, 0, CUT, 0, 0, CUT)[i]
-        src = res.at[code_rows(owner, lo)] if i < 4 else code_sum.at[i - 4]
+        if i < 4:
+            owner = (opposite, opposite, pair, next_)[i]
+            src = res.at[code_rows(owner, (CUT, 0, CUT, 0)[i], CUT)]
+        else:
+            src = code_sum.at[i % 2, pl.ds(i // 6 * PART, PART)]
         return pltpu.make_async_remote_copy(
             src_ref=src,
             dst_ref=code_got(i),
             send_sem=c_send.at[i],
             recv_sem=c_recv.at[i],
-            device_id={"replica": peer},
+            device_id={"replica": (pair, next_)[i % 2]},
             device_id_type=MESH,
         )
 
@@ -497,8 +502,10 @@
     def code_pass(i):
         code_copy(1 - i).wait_recv()
         owner, lo = ((pair, 0), (next_, CUT))[i]
-        code_sum[i] = (res[code_rows(owner, lo), :].astype(F32) + code_got(1 - i)[...].astype(F32)).astype(BF16)
+        own_codes = res[code_rows(owner, lo, CUT), :].astype(F32)
+        code_sum[i] = (own_codes + code_got(1 - i)[...].astype(F32)).astype(BF16)
         code_copy(4 + i).start()
+        code_copy(6 + i).start()
 
     weights_wait(10)
     partial(1, 0)
@@ -539,22 +546,24 @@
     results.append(pltpu.make_async_copy(grad_in_ref, grad_in_hbm, l_sem.at[8]))
     results[1].start()
 
-    for lo, first, second in ((0, 3, 4), (CUT, 2, 5)):
-        code_copy(first).wait_recv()
+    code_copy(2).wait_recv()
+    code_copy(3).wait_recv()
+    for at, first, second in ((0, 3, 4), (2, 2, 5), (1, 3, 6), (3, 2, 7)):
         code_copy(second).wait_recv()
-
-        def add_codes(t, _, lo=lo, first=first, second=second):
-            rows = pl.ds(pl.multiple_of(lo + t * 64, 64), 64)
-            total = res[pl.ds(pl.multiple_of(y * SHARD + lo + t * 64, 64), 64), :].astype(F32)
-            for i in (first, second):
-                got = pl.ds(pl.multiple_of(i % 2 * CUT + t * 64, 64), 64)
-                total = total + wf[0, i // 2, got, :].astype(F32)
+        lo = at * PART
+
+        def add_codes(t, _, lo=lo, first=first):
+            rows = pl.ds(pl.multiple_of(lo + t * 32, 32), 32)
+            total = res[pl.ds(pl.multiple_of(y * SHARD + lo + t * 32, 32), 32), :].astype(F32)
+            part_of = lo % CUT + t * 32
+            total = total + wf[0, 1, pl.ds(pl.multiple_of(first % 2 * CUT + part_of, 32), 32), :].astype(F32)
+            total = total + wf[0, 2, pl.ds(pl.multiple_of((1 - first % 2) * CUT + part_of, 32), 32), :].astype(F32)
             sums_ref[rows, :] = total
             return 0
 
-        lax.fori_loop(0, CUT // 64, add_codes, 0)
-        rows = pl.ds(lo, CUT)
-        results.append(pltpu.make_async_copy(sums_ref.at[rows], sums_hbm.at[rows], l_sem.at[9 + lo // CUT]))
+        lax.fori_loop(0, PART // 32, add_codes, 0)
+        rows = pl.ds(lo, PART)
+        results.append(pltpu.make_async_copy(sums_ref.at[rows], sums_hbm.at[rows], l_sem.at[9 + at]))
         results[-1].start()
 
     for number in range(18):
@@ -565,7 +574,7 @@
     for r in range(7):
         for way in range(2):
             ring_copy(way, r).wait_send()
-    for i in range(6):
+    for i in range(8):
         code_copy(i).wait_send()
     for stage, half in ((0, near), (1, 1 - near)):
         @pl.when(half != core)
@@ -657,9 +666,9 @@
             dma((8,)),
             dma((3,)),
             dma((3,)),
-            dma((6,)),
-            dma((6,)),
-            dma((11,)),
+            dma((8,)),
+            dma((8,)),
+            dma((13,)),
         ],
         compiler_params=pltpu.CompilerParams(
             collective_id=0, has_side_effects=True, vmem_limit_bytes=62 * 2**20

time: 142 us -> 141 us (level)
  no operation moved by 1% of the time
where the time goes in v6:
time: 141 us
  Pallas kernels  141 us (100%)
    pallas_call x1, Pallas kernels, local(): pl.pallas_call(kernel, out_shape=(jax.ShapeDtypeStruct((TOKENS, HALF_D),...  138 us

profile of v6, /device:TPU:1, one launch (start us, length us, event | category | flops | bytes accessed | tf_op | source)
XLA Modules:
  0.0 141.3 jit_solution(10648326545521351237)
XLA Ops:
  0.6 138.0 %shard_map.112 = (bf16[128,1792]{1,0:T(8,128)(2,1)}, f32[896,512]{1,0:T(8,128)}, f32[28,512]{1,0:T(8,128)}) custom-call(s32[4,128]{1,0:T(4,128)} %bitcast.18, f32[4,128]{1,0:T(4,128)} %bitcast.19, bf16[128,3584]{1,0:T(8,128)(2,1)} %grad_hbm.1, bf16[32,24,512]{2,1,0:T(8,128)(2,1)} %bitcast.15, bf16[32,24,512]{2,1,0:T(8,128)(2,1)} %bitcast.16, ...), custom_call_target="tpu_custom_call" | custom-call | flops 11299999744 | bytes 14000000 | tf_op jit(solution)/shard_map/pallas_call | solution.py:616
  138.7 2.6 %shard_map.113 = (bf16[128,1792]{1,0:T(8,128)(2,1)}, f32[896,512]{1,0:T(8,128)}, f32[28,1,512]{2,1,0:T(1,128)}) custom-call(bf16[128,1792]{1,0:T(8,128)(2,1)} %get-tuple-element.9.grad_ref, f32[896,512]{1,0:T(8,128)} %get-tuple-element.10.sums_ref, f32[28,512]{1,0:T(8,128)} %get-tuple-element.11.scales_ref), custom_call_target="tpu_custom_call" | custom-call | tf_op jit(solution)/shard_map/pallas_call | solution.py:680
